TPU v7x, 32 devices: a whole 2x2x4 slice. The times are simulated.
32 devices in a mesh: ctx: 8 (over z, y), tp: 4 (over x, core).
Axes of the slice: x: 2, y: 2, z: 4, core: 2. Of those that a mesh axis runs over, the one named last changes fastest.
Arguments:
- queries: bfloat16 [6144, 2048], P('ctx', 'tp'), may hold values from -6 to 6
- keys: bfloat16 [6144, 2048], P('ctx', 'tp'), may hold values from -6 to 6
- values: bfloat16 [6144, 2048], P('ctx', 'tp'), may hold values from -6 to 6
- out_grad: bfloat16 [6144, 2048], P('ctx', 'tp'), may hold values from -6 to 6
- key_blocks: int32 [24, 16], replicated, may hold values from -1 to 23, as said below
- target_counts: int32 [24], replicated, may hold values from 0 to 128, as said below
Outputs:
- query_grad: bfloat16 [6144, 2048], P('ctx', 'tp')
- key_grad: bfloat16 [6144, 2048], P('ctx', 'tp')
- value_grad: bfloat16 [6144, 2048], P('ctx', 'tp')
Inputs may be any that keep to these rules, and one draw needn't show every extreme that they name: `key_blocks`: entry 0 of row b is b itself; the other entries are distinct blocks k with b - 6 <= k < b, or -1 for an empty slot; a row has empty slots only where fewer than 15 such blocks exist. The last target_counts[b] events of block b are targets: no other event reads them as keys.
All inputs are finite; a program needn't handle non-finite values.
Results may differ from a plain program's by a relative error of at most 0.005.
Values may be sent and summed in bfloat16 or wider, within the bound.
A program may use at most 64 MiB of HBM per device.

v0:
```python
import math

import jax
import jax.numpy as jnp
from jax import lax
from jax.sharding import PartitionSpec as P

HEAD = 128
BLK = 256
KPB = 16


def from_behind(array, axis, by):
    length = lax.axis_size(axis)
    pairs = [(i, i + by) for i in range(length) if 0 <= i + by < length]
    return lax.ppermute(array, axis, pairs)


def passed_along(array, axis, by):
    length = lax.axis_size(axis)
    return lax.ppermute(array, axis, [(i, (i + by) % length) for i in range(length)])


def block_mask(query_id, key_id, target_counts):
    row_index = jnp.arange(BLK, dtype=jnp.int32)[:, None]
    col_index = jnp.arange(BLK, dtype=jnp.int32)[None, :]
    own_targets = target_counts[query_id]
    key_targets = target_counts[key_id]
    diagonal = (col_index <= row_index) & (
        (col_index < BLK - own_targets) | (col_index == row_index)
    )
    earlier = jnp.broadcast_to(col_index < BLK - key_targets, diagonal.shape)
    return jnp.where(query_id == key_id, diagonal, earlier).astype(jnp.float32)


def tile_grads(query_tile, grad_tile, key_tile, value_tile, allowed):
    head_factor = 1.0 / math.sqrt(HEAD)
    norm_scale = 1.0 / math.sqrt(KPB * BLK)
    scores = (
        jnp.einsum("ihd,jhd->hij", query_tile, key_tile, preferred_element_type=jnp.float32)
        * head_factor
    )
    sigmoid_part = jax.nn.sigmoid(scores)
    gated = allowed[None] * norm_scale
    weights = (scores * sigmoid_part * gated).astype(jnp.bfloat16)
    weight_grad = jnp.einsum(
        "ihd,jhd->hij", grad_tile, value_tile, preferred_element_type=jnp.float32
    )
    score_grad = (
        weight_grad * gated * sigmoid_part * (1.0 + scores * (1.0 - sigmoid_part))
    ).astype(jnp.bfloat16)
    query_part = (
        jnp.einsum("hij,jhd->ihd", score_grad, key_tile, preferred_element_type=jnp.float32)
        * head_factor
    )
    key_part = (
        jnp.einsum("hij,ihd->jhd", score_grad, query_tile, preferred_element_type=jnp.float32)
        * head_factor
    )
    payload_portion = jnp.einsum(
        "hij,ihd->jhd", weights, grad_tile, preferred_element_type=jnp.float32
    )
    return (query_part, key_part, payload_portion)


def visit(
    query_base,
    key_base,
    active,
    query_here,
    grad_here,
    key_here,
    value_here,
    grads,
    key_blocks,
    target_counts,
):
    per_device = query_here.shape[0]
    total_blocks = key_blocks.shape[0]

    def pair_step(pair_index, present_value):
        query_slot = pair_index // per_device
        key_slot = pair_index % per_device
        query_id = jnp.clip(query_base + query_slot, 0, total_blocks - 1)
        key_id = key_base + key_slot
        listed = active & jnp.any(key_blocks[query_id] == key_id)

        def work(accums):
            query_acc, key_acc, value_acc = accums
            safe_key = jnp.clip(key_id, 0, total_blocks - 1)
            allowed = block_mask(query_id, safe_key, target_counts)
            query_part, key_part, payload_portion = tile_grads(
                query_here[query_slot],
                grad_here[query_slot],
                key_here[key_slot],
                value_here[key_slot],
                allowed,
            )
            return (
                query_acc.at[query_slot].add(query_part),
                key_acc.at[key_slot].add(key_part),
                value_acc.at[key_slot].add(payload_portion),
            )

        return lax.cond(listed, work, lambda unchanged: unchanged, present_value)

    return lax.fori_loop(0, per_device * per_device, pair_step, grads)


def body(queries, keys, values, out_grad, key_blocks, target_counts):
    cycle_size = lax.axis_size("ctx")
    reach_hops = cycle_size // 4
    position = lax.axis_index("ctx")
    per_device = queries.shape[0] // BLK
    heads_here = queries.shape[1] // HEAD
    block_shape = (per_device, BLK, heads_here, HEAD)
    query_blocks = queries.reshape(block_shape)
    key_tiles = keys.reshape(block_shape)
    value_tiles = values.reshape(block_shape)
    grad_blocks = out_grad.reshape(block_shape)
    empty = jnp.zeros(block_shape, jnp.float32)

    def query_hop(hop_index, state):
        query_here, grad_here, query_acc, key_acc, value_acc = state
        source = position + hop_index
        query_acc, key_acc, value_acc = visit(
            source * per_device,
            position * per_device,
            source < cycle_size,
            query_here,
            grad_here,
            key_tiles,
            value_tiles,
            (query_acc, key_acc, value_acc),
            key_blocks,
            target_counts,
        )
        query_here, grad_here = from_behind((query_here, grad_here), "ctx", -1)
        query_acc = passed_along(query_acc, "ctx", -1)
        return (query_here, grad_here, query_acc, key_acc, value_acc)

    state = lax.fori_loop(
        0, reach_hops, query_hop, (query_blocks, grad_blocks, empty, empty, empty)
    )
    query_here, grad_here, query_acc, key_acc, value_acc = state
    source = position + reach_hops
    query_acc, key_acc, value_acc = visit(
        source * per_device,
        position * per_device,
        source < cycle_size,
        query_here,
        grad_here,
        key_tiles,
        value_tiles,
        (query_acc, key_acc, value_acc),
        key_blocks,
        target_counts,
    )
    query_acc = passed_along(query_acc.astype(jnp.bfloat16), "ctx", reach_hops).astype(
        query_acc.dtype
    )
    flat = queries.shape
    return (
        query_acc.reshape(flat).astype(jnp.bfloat16),
        key_acc.reshape(flat).astype(jnp.bfloat16),
        value_acc.reshape(flat).astype(jnp.bfloat16),
    )


def solution(mesh):
    in_specs = (P("ctx", "tp"), P("ctx", "tp"), P("ctx", "tp"), P("ctx", "tp"), P(), P())
    out_specs = (P("ctx", "tp"), P("ctx", "tp"), P("ctx", "tp"))
    return jax.shard_map(body, mesh=mesh, in_specs=in_specs, out_specs=out_specs, check_vma=False)
```

profile of v0, /device:TPU:10, one launch (start us, length us, event | category | flops | bytes accessed | tf_op | source)
XLA Modules:
  0.0 426.8 jit_solution(8001798551420042587)
XLA Ops:
  9.0 313.5 %while.90 = (s32[]{:T(128)}, bf16[3,256,4,128]{3,1,2,0:T(8,128)(2,1)}, bf16[3,256,4,128]{3,1,2,0:T(8,128)(2,1)}, f32[3,256,4,128]{1,3,2,0:T(8,128)S(1)}, f32[3,2...) while((s32[]{:T(128)}, ...), condition=%wide.region_8.9_spmd, body=%wide.region_0.8_spmd.sunk | while | flops 341443200 | bytes 57675284 | solution.py:142
  12.2 69.5 %while.92 = (s32[]{:T(128)}, f32[3,256,4,128]{1,3,2,0:T(8,128)S(1)}, f32[3,256,4,128]{1,3,2,0:T(8,128)}, f32[3,256,4,128]{1,3,2,0:T(8,128)}, s32[]{:T(128)}, /*i...) while((s32[]{:T(128)}, ...), condition=%wide.region_7.7_spmd, body=%wide.region_1.6_spmd.sunk | while | flops 341443200 | bytes 38800408 | solution.py:107
  27.3 9.5 %conditional.5 = ((f32[3,256,4,128]{1,3,2,0:T(8,128)S(1)}, f32[3,256,4,128]{1,3,2,0:T(8,128)}, f32[3,256,4,128]{1,3,2,0:T(8,128)})) conditional(s32[]{:T(128)} %convert_element_type.70, (f32[3,256,4,128]{1,3,2,0:T(8,128)S(1)}, f32[3,256,4,128]{1,3,2,0:T(8,128)}, f32[3,256,4,128]{1,3,2,0:T(8,128)}) %tuple.161, (s32[]{:T(128)}, ...), branch_computations={%region_3.2_spmd, %region_4.5_spmd} | conditional | flops 341443136 | bytes 38799880 | solution.py:105
  92.1 27.1 %collective-permute-done.2 = f32[3,256,4,128]{1,3,2,0:T(8,128)} collective-permute-done((f32[3,256,4,128]{1,3,2,0:T(8,128)S(1)}, f32[3,256,4,128]{1,3,2,0:T(8,128)}, u32[]{:S(2)}, u32[]{:S(2)}) %collective-permute-start.2) | collective-permute-done | bytes 1572896 | tf_op jit(solution)/shard_map/while/body/eval_jaxpr/ppermute | solution.py:21
  120.6 15.4 %collective-permute-done = bf16[3,256,4,128]{3,1,2,0:T(8,128)(2,1)} collective-permute-done((bf16[3,256,4,128]{3,1,2,0:T(8,128)(2,1)S(1)}, bf16[3,256,4,128]{3,1,2,0:T(8,128)(2,1)}, u32[]{:S(2)}, u32[]{:S(2)}) %collective-permute-start) | collective-permute-done | bytes 786464 | tf_op jit(solution)/shard_map/while/body/eval_jaxpr/ppermute | solution.py:16
  136.0 15.7 %collective-permute-done.1 = bf16[3,256,4,128]{3,1,2,0:T(8,128)(2,1)} collective-permute-done((bf16[3,256,4,128]{3,1,2,0:T(8,128)(2,1)}, bf16[3,256,4,128]{3,1,2,0:T(8,128)(2,1)}, u32[]{:S(2)}, u32[]{:S(2)}) %collective-permute-start.1) | collective-permute-done | bytes 786464 | tf_op jit(solution)/shard_map/while/body/eval_jaxpr/ppermute | solution.py:16
  154.9 97.9 %while.92 = (s32[]{:T(128)}, f32[3,256,4,128]{1,3,2,0:T(8,128)S(1)}, f32[3,256,4,128]{1,3,2,0:T(8,128)}, f32[3,256,4,128]{1,3,2,0:T(8,128)}, s32[]{:T(128)}, /*i...) while((s32[]{:T(128)}, ...), condition=%wide.region_7.7_spmd, body=%wide.region_1.6_spmd.sunk | while | flops 341443200 | bytes 38800408 | solution.py:107
  188.9 9.5 %conditional.5 = ((f32[3,256,4,128]{1,3,2,0:T(8,128)S(1)}, f32[3,256,4,128]{1,3,2,0:T(8,128)}, f32[3,256,4,128]{1,3,2,0:T(8,128)})) conditional(s32[]{:T(128)} %convert_element_type.70, (f32[3,256,4,128]{1,3,2,0:T(8,128)S(1)}, f32[3,256,4,128]{1,3,2,0:T(8,128)}, f32[3,256,4,128]{1,3,2,0:T(8,128)}) %tuple.161, (s32[]{:T(128)}, ...), branch_computations={%region_3.2_spmd, %region_4.5_spmd} | conditional | flops 341443136 | bytes 38799880 | solution.py:105
  199.8 9.5 %conditional.5 = ((f32[3,256,4,128]{1,3,2,0:T(8,128)S(1)}, f32[3,256,4,128]{1,3,2,0:T(8,128)}, f32[3,256,4,128]{1,3,2,0:T(8,128)})) conditional(s32[]{:T(128)} %convert_element_type.70, (f32[3,256,4,128]{1,3,2,0:T(8,128)S(1)}, f32[3,256,4,128]{1,3,2,0:T(8,128)}, f32[3,256,4,128]{1,3,2,0:T(8,128)}) %tuple.161, (s32[]{:T(128)}, ...), branch_computations={%region_3.2_spmd, %region_4.5_spmd} | conditional | flops 341443136 | bytes 38799880 | solution.py:105
  210.6 9.5 %conditional.5 = ((f32[3,256,4,128]{1,3,2,0:T(8,128)S(1)}, f32[3,256,4,128]{1,3,2,0:T(8,128)}, f32[3,256,4,128]{1,3,2,0:T(8,128)})) conditional(s32[]{:T(128)} %convert_element_type.70, (f32[3,256,4,128]{1,3,2,0:T(8,128)S(1)}, f32[3,256,4,128]{1,3,2,0:T(8,128)}, f32[3,256,4,128]{1,3,2,0:T(8,128)}) %tuple.161, (s32[]{:T(128)}, ...), branch_computations={%region_3.2_spmd, %region_4.5_spmd} | conditional | flops 341443136 | bytes 38799880 | solution.py:105
  221.5 9.5 %conditional.5 = ((f32[3,256,4,128]{1,3,2,0:T(8,128)S(1)}, f32[3,256,4,128]{1,3,2,0:T(8,128)}, f32[3,256,4,128]{1,3,2,0:T(8,128)})) conditional(s32[]{:T(128)} %convert_element_type.70, (f32[3,256,4,128]{1,3,2,0:T(8,128)S(1)}, f32[3,256,4,128]{1,3,2,0:T(8,128)}, f32[3,256,4,128]{1,3,2,0:T(8,128)}) %tuple.161, (s32[]{:T(128)}, ...), branch_computations={%region_3.2_spmd, %region_4.5_spmd} | conditional | flops 341443136 | bytes 38799880 | solution.py:105
  232.4 9.5 %conditional.5 = ((f32[3,256,4,128]{1,3,2,0:T(8,128)S(1)}, f32[3,256,4,128]{1,3,2,0:T(8,128)}, f32[3,256,4,128]{1,3,2,0:T(8,128)})) conditional(s32[]{:T(128)} %convert_element_type.70, (f32[3,256,4,128]{1,3,2,0:T(8,128)S(1)}, f32[3,256,4,128]{1,3,2,0:T(8,128)}, f32[3,256,4,128]{1,3,2,0:T(8,128)}) %tuple.161, (s32[]{:T(128)}, ...), branch_computations={%region_3.2_spmd, %region_4.5_spmd} | conditional | flops 341443136 | bytes 38799880 | solution.py:105
  243.3 9.5 %conditional.5 = ((f32[3,256,4,128]{1,3,2,0:T(8,128)S(1)}, f32[3,256,4,128]{1,3,2,0:T(8,128)}, f32[3,256,4,128]{1,3,2,0:T(8,128)})) conditional(s32[]{:T(128)} %convert_element_type.70, (f32[3,256,4,128]{1,3,2,0:T(8,128)S(1)}, f32[3,256,4,128]{1,3,2,0:T(8,128)}, f32[3,256,4,128]{1,3,2,0:T(8,128)}) %tuple.161, (s32[]{:T(128)}, ...), branch_computations={%region_3.2_spmd, %region_4.5_spmd} | conditional | flops 341443136 | bytes 38799880 | solution.py:105
  259.0 31.7 %collective-permute-done.2 = f32[3,256,4,128]{1,3,2,0:T(8,128)} collective-permute-done((f32[3,256,4,128]{1,3,2,0:T(8,128)S(1)}, f32[3,256,4,128]{1,3,2,0:T(8,128)}, u32[]{:S(2)}, u32[]{:S(2)}) %collective-permute-start.2) | collective-permute-done | bytes 1572896 | tf_op jit(solution)/shard_map/while/body/eval_jaxpr/ppermute | solution.py:21
  292.0 15.4 %collective-permute-done = bf16[3,256,4,128]{3,1,2,0:T(8,128)(2,1)} collective-permute-done((bf16[3,256,4,128]{3,1,2,0:T(8,128)(2,1)S(1)}, bf16[3,256,4,128]{3,1,2,0:T(8,128)(2,1)}, u32[]{:S(2)}, u32[]{:S(2)}) %collective-permute-start) | collective-permute-done | bytes 786464 | tf_op jit(solution)/shard_map/while/body/eval_jaxpr/ppermute | solution.py:16
  307.5 15.1 %collective-permute-done.1 = bf16[3,256,4,128]{3,1,2,0:T(8,128)(2,1)} collective-permute-done((bf16[3,256,4,128]{3,1,2,0:T(8,128)(2,1)}, bf16[3,256,4,128]{3,1,2,0:T(8,128)(2,1)}, u32[]{:S(2)}, u32[]{:S(2)}) %collective-permute-start.1) | collective-permute-done | bytes 786464 | tf_op jit(solution)/shard_map/while/body/eval_jaxpr/ppermute | solution.py:16
  322.5 82.7 %while.91 = (s32[]{:T(128)}, f32[3,256,4,128]{1,3,2,0:T(8,128)S(1)}, f32[3,256,4,128]{1,3,2,0:T(8,128)}, f32[3,256,4,128]{1,3,2,0:T(8,128)}, s32[]{:T(128)}, /*i...) while((s32[]{:T(128)}, ...), condition=%wide.region_15.16_spmd, body=%wide.region_9.15_spmd.sunk | while | flops 341443200 | bytes 35658724 | solution.py:107
  323.8 11.8 %conditional.4 = ((f32[3,256,4,128]{1,3,2,0:T(8,128)S(1)}, f32[3,256,4,128]{1,3,2,0:T(8,128)}, f32[3,256,4,128]{1,3,2,0:T(8,128)})) conditional(s32[]{:T(128)} %convert_element_type.69, (f32[3,256,4,128]{1,3,2,0:T(8,128)S(1)}, f32[3,256,4,128]{1,3,2,0:T(8,128)}, f32[3,256,4,128]{1,3,2,0:T(8,128)}) %tuple.158, (s32[]{:T(128)}, ...), branch_computations={%region_11.11_spmd, %region_12.14_spmd} | conditional | flops 341443136 | bytes 35658196 | solution.py:105
  336.9 11.8 %conditional.4 = ((f32[3,256,4,128]{1,3,2,0:T(8,128)S(1)}, f32[3,256,4,128]{1,3,2,0:T(8,128)}, f32[3,256,4,128]{1,3,2,0:T(8,128)})) conditional(s32[]{:T(128)} %convert_element_type.69, (f32[3,256,4,128]{1,3,2,0:T(8,128)S(1)}, f32[3,256,4,128]{1,3,2,0:T(8,128)}, f32[3,256,4,128]{1,3,2,0:T(8,128)}) %tuple.158, (s32[]{:T(128)}, ...), branch_computations={%region_11.11_spmd, %region_12.14_spmd} | conditional | flops 341443136 | bytes 35658196 | solution.py:105
  350.0 11.8 %conditional.4 = ((f32[3,256,4,128]{1,3,2,0:T(8,128)S(1)}, f32[3,256,4,128]{1,3,2,0:T(8,128)}, f32[3,256,4,128]{1,3,2,0:T(8,128)})) conditional(s32[]{:T(128)} %convert_element_type.69, (f32[3,256,4,128]{1,3,2,0:T(8,128)S(1)}, f32[3,256,4,128]{1,3,2,0:T(8,128)}, f32[3,256,4,128]{1,3,2,0:T(8,128)}) %tuple.158, (s32[]{:T(128)}, ...), branch_computations={%region_11.11_spmd, %region_12.14_spmd} | conditional | flops 341443136 | bytes 35658196 | solution.py:105
  364.5 11.8 %conditional.4 = ((f32[3,256,4,128]{1,3,2,0:T(8,128)S(1)}, f32[3,256,4,128]{1,3,2,0:T(8,128)}, f32[3,256,4,128]{1,3,2,0:T(8,128)})) conditional(s32[]{:T(128)} %convert_element_type.69, (f32[3,256,4,128]{1,3,2,0:T(8,128)S(1)}, f32[3,256,4,128]{1,3,2,0:T(8,128)}, f32[3,256,4,128]{1,3,2,0:T(8,128)}) %tuple.158, (s32[]{:T(128)}, ...), branch_computations={%region_11.11_spmd, %region_12.14_spmd} | conditional | flops 341443136 | bytes 35658196 | solution.py:105
  377.6 11.8 %conditional.4 = ((f32[3,256,4,128]{1,3,2,0:T(8,128)S(1)}, f32[3,256,4,128]{1,3,2,0:T(8,128)}, f32[3,256,4,128]{1,3,2,0:T(8,128)})) conditional(s32[]{:T(128)} %convert_element_type.69, (f32[3,256,4,128]{1,3,2,0:T(8,128)S(1)}, f32[3,256,4,128]{1,3,2,0:T(8,128)}, f32[3,256,4,128]{1,3,2,0:T(8,128)}) %tuple.158, (s32[]{:T(128)}, ...), branch_computations={%region_11.11_spmd, %region_12.14_spmd} | conditional | flops 341443136 | bytes 35658196 | solution.py:105
  393.4 11.8 %conditional.4 = ((f32[3,256,4,128]{1,3,2,0:T(8,128)S(1)}, f32[3,256,4,128]{1,3,2,0:T(8,128)}, f32[3,256,4,128]{1,3,2,0:T(8,128)})) conditional(s32[]{:T(128)} %convert_element_type.69, (f32[3,256,4,128]{1,3,2,0:T(8,128)S(1)}, f32[3,256,4,128]{1,3,2,0:T(8,128)}, f32[3,256,4,128]{1,3,2,0:T(8,128)}) %tuple.158, (s32[]{:T(128)}, ...), branch_computations={%region_11.11_spmd, %region_12.14_spmd} | conditional | flops 341443136 | bytes 35658196 | solution.py:105
  411.4 12.9 %collective-permute-done.3 = bf16[3,256,4,128]{1,3,2,0:T(8,128)(2,1)} collective-permute-done((bf16[3,256,4,128]{1,3,2,0:T(8,128)(2,1)}, bf16[3,256,4,128]{1,3,2,0:T(8,128)(2,1)}, u32[]{:S(2)}, u32[]{:S(2)}) %collective-permute-start.3) | collective-permute-done | bytes 786464 | tf_op jit(solution)/shard_map/ppermute | solution.py:21
  (516 shorter events, 323.5 us)
Async XLA Ops:
  6.4 2.6 copy-start.6
  6.4 2.6 copy-start.12
  81.8 37.4 %collective-permute-start.2 = (f32[3,256,4,128]{1,3,2,0:T(8,128)S(1)}, f32[3,256,4,128]{1,3,2,0:T(8,128)}, u32[]{:S(2)}, u32[]{:S(2)}) collective-permute-start(f32[3,256,4,128]{1,3,2,0:T(8,128)S(1)} %get-tuple-element.1505), channel_id=1, source_target_pairs={{0,28},{4,0},{8,4},{12,8},{16,12},{20,16},{24,20},{28,24},{1,29},{... | collective-permute-start | bytes 4718600 | tf_op jit(solution)/shard_map/while/body/eval_jaxpr/ppermute | solution.py:21
  83.2 52.8 %collective-permute-start = (bf16[3,256,4,128]{3,1,2,0:T(8,128)(2,1)S(1)}, bf16[3,256,4,128]{3,1,2,0:T(8,128)(2,1)}, u32[]{:S(2)}, u32[]{:S(2)}) collective-permute-start(bf16[3,256,4,128]{3,1,2,0:T(8,128)(2,1)S(1)} %get-tuple-element.1726), channel_id=1, source_target_pairs={{4,0},{8,4},{12,8},{16,12},{20,16},{24,20},{28,24},{5,1},{9,5},{13... | collective-permute-start | bytes 2359304 | tf_op jit(solution)/shard_map/while/body/eval_jaxpr/ppermute | solution.py:16
  85.6 66.1 %collective-permute-start.1 = (bf16[3,256,4,128]{3,1,2,0:T(8,128)(2,1)}, bf16[3,256,4,128]{3,1,2,0:T(8,128)(2,1)}, u32[]{:S(2)}, u32[]{:S(2)}) collective-permute-start(bf16[3,256,4,128]{3,1,2,0:T(8,128)(2,1)} %get-tuple-element.1735), channel_id=1, source_target_pairs={{4,0},{8,4},{12,8},{16,12},{20,16},{24,20},{28,24},{5,1},{9,5},{13... | collective-permute-start | bytes 2359304 | tf_op jit(solution)/shard_map/while/body/eval_jaxpr/ppermute | solution.py:16
  252.8 37.8 %collective-permute-start.2 = (f32[3,256,4,128]{1,3,2,0:T(8,128)S(1)}, f32[3,256,4,128]{1,3,2,0:T(8,128)}, u32[]{:S(2)}, u32[]{:S(2)}) collective-permute-start(f32[3,256,4,128]{1,3,2,0:T(8,128)S(1)} %get-tuple-element.1505), channel_id=1, source_target_pairs={{0,28},{4,0},{8,4},{12,8},{16,12},{20,16},{24,20},{28,24},{1,29},{... | collective-permute-start | bytes 4718600 | tf_op jit(solution)/shard_map/while/body/eval_jaxpr/ppermute | solution.py:21
  255.1 52.4 %collective-permute-start = (bf16[3,256,4,128]{3,1,2,0:T(8,128)(2,1)S(1)}, bf16[3,256,4,128]{3,1,2,0:T(8,128)(2,1)}, u32[]{:S(2)}, u32[]{:S(2)}) collective-permute-start(bf16[3,256,4,128]{3,1,2,0:T(8,128)(2,1)S(1)} %get-tuple-element.1726), channel_id=1, source_target_pairs={{4,0},{8,4},{12,8},{16,12},{20,16},{24,20},{28,24},{5,1},{9,5},{13... | collective-permute-start | bytes 2359304 | tf_op jit(solution)/shard_map/while/body/eval_jaxpr/ppermute | solution.py:16
  257.0 65.5 %collective-permute-start.1 = (bf16[3,256,4,128]{3,1,2,0:T(8,128)(2,1)}, bf16[3,256,4,128]{3,1,2,0:T(8,128)(2,1)}, u32[]{:S(2)}, u32[]{:S(2)}) collective-permute-start(bf16[3,256,4,128]{3,1,2,0:T(8,128)(2,1)} %get-tuple-element.1735), channel_id=1, source_target_pairs={{4,0},{8,4},{12,8},{16,12},{20,16},{24,20},{28,24},{5,1},{9,5},{13... | collective-permute-start | bytes 2359304 | tf_op jit(solution)/shard_map/while/body/eval_jaxpr/ppermute | solution.py:16
  327.0 2.4 copy-start.2
  329.4 3.0 copy-start.9
  331.4 3.1 copy-start.3
  340.1 2.4 copy-start.2
  342.6 3.0 copy-start.9
  344.5 3.1 copy-start.3
  355.7 3.0 copy-start.9
  357.6 3.1 copy-start.3
  370.1 3.0 copy-start.9
  372.1 3.1 copy-start.3
  383.2 3.0 copy-start.9
  385.2 3.1 copy-start.3
  399.0 3.0 copy-start.9
  401.0 3.1 copy-start.3
  405.2 2.6 copy-start.4
  406.2 18.1 %collective-permute-start.3 = (bf16[3,256,4,128]{1,3,2,0:T(8,128)(2,1)}, bf16[3,256,4,128]{1,3,2,0:T(8,128)(2,1)}, u32[]{:S(2)}, u32[]{:S(2)}) collective-permute-start(bf16[3,256,4,128]{1,3,2,0:T(8,128)(2,1)} %convert_element_type.55), channel_id=1, source_target_pairs={{0,8},{4,12},{8,16},{12,20},{16,24},{20,28},{24,0},{28,4},{1,9},{5... | collective-permute-start | bytes 2359304 | tf_op jit(solution)/shard_map/ppermute | solution.py:21
  (110 other events, 184.1 us)
where the time goes:
time: 434 us; the launch traced here: 427 us
  waiting for transfers between devices  133 us (31%)
  matrix products  120 us (28%)
  local copies, waits for them, and re-layouts  72.5 us (17%)
  loops' own time  45.4 us (10%)
  other arithmetic  36.7 us (8%)
  starting transfers between devices  18 us (4%)
    ppermute x3, waiting for transfers between devices, passed_along(): lax.ppermute(array, axis, [(i, (i + by) % length) for i in range(length)])  71.7 us
    ppermute x4, waiting for transfers between devices, from_behind(): return lax.ppermute(array, axis, pairs)  61.7 us
    cond x240, local copies, waits for them, and re-layouts  36.4 us
    dot_general x21, matrix products, tile_grads(): jnp.einsum('ihd,jhd->hij', grad_tile, value_tile, preferred_element_type=...  34 us
    dot_general x21, matrix products, tile_grads(): jnp.einsum('hij,ihd->jhd', weights, grad_tile, preferred_element_type=jnp...  28.6 us
    another operation x27, loops' own time, pair_step(): return lax.cond(listed, work, lambda unchanged: unchanged, present_value)  28.4 us
    dot_general x21, matrix products, tile_grads(): jnp.einsum('hij,ihd->jhd', score_grad, query_tile, preferred_element_type...  26.5 us
    reduce_or x27, other arithmetic, pair_step(): listed = active & jnp.any(key_blocks[query_id] == key_id)  19.2 us
  transfers between devices with their start and end apart: 7, of which 7 were waited for; matrix products, arithmetic and copies ran while one was open for 1% of the time, Pallas kernels for 0%

commit v1 on v0

--- a/solution.py
+++ b/solution.py
@@ -1,13 +1,254 @@
+import functools
 import math
 
 import jax
 import jax.numpy as jnp
 from jax import lax
+from jax.experimental import pallas as pl
+from jax.experimental.pallas import tpu as pltpu
 from jax.sharding import PartitionSpec as P
 
 HEAD = 128
 BLK = 256
 KPB = 16
+MESH = pl.DeviceIdType.MESH
+HEAD_FACTOR = 1.0 / math.sqrt(HEAD)
+NORM_SCALE = 1.0 / math.sqrt(KPB * BLK)
+
+
+def nt(a, b):
+    return lax.dot_general(a, b, (((1,), (1,)), ((), ())), preferred_element_type=jnp.float32)
+
+
+def tn(a, b):
+    return lax.dot_general(a, b, (((0,), (0,)), ((), ())), preferred_element_type=jnp.float32)
+
+
+def tile(query, grad, key, value, allowed=None):
+    half = nt(key, query) * (0.5 * HEAD_FACTOR)
+    one_tanh = 1.0 + jnp.tanh(half)
+    weights = half * one_tanh
+    score_grad = nt(value, grad) * (one_tanh * ((1.0 + (half + half)) - weights))
+    if allowed is not None:
+        weights = jnp.where(allowed, weights, 0.0)
+        score_grad = jnp.where(allowed, score_grad, 0.0)
+    weights = weights.astype(jnp.bfloat16)
+    score_grad = score_grad.astype(jnp.bfloat16)
+    value_part = jnp.dot(weights, grad, preferred_element_type=jnp.float32)
+    key_part = jnp.dot(score_grad, query, preferred_element_type=jnp.float32)
+    query_part = tn(score_grad, key)
+    return query_part, key_part, value_part
+
+
+def kernel(
+    n, per, heads,
+    blocks_ref, counts_ref, q_ref, g_ref, k_ref, v_ref,
+    dq_ref, dk_ref, dv_ref,
+    r1q, r1g, r2q, r2g, dq1, dq2, rq1, rq2, dq0, dk_acc, dv_acc, mask,
+    z_send, z_recv, y_send, y_recv, d1_send, d1_recv, d2_send, d2_recv,
+):
+    p = lax.axis_index("ctx")
+    total = n * per
+    odd = lax.rem(p, 2) == 1
+    even = lax.rem(p, 2) == 0
+    has1, has2 = p + 1 < n, p + 2 < n
+    back1, back2 = p >= 1, p >= 2
+    next1, next2 = lax.rem(p + 1, n), lax.rem(p + 2, n)
+    prev1, prev2 = lax.rem(p + n - 1, n), lax.rem(p + n - 2, n)
+    partner = p + 1 - 2 * lax.rem(p, 2)
+    chunks = heads * per
+    dq_scale = 0.5 * NORM_SCALE * HEAD_FACTOR
+
+    def part(ref, c):
+        rows = pl.ds(pl.multiple_of(lax.rem(c, per) * BLK, BLK), BLK)
+        cols = pl.ds(pl.multiple_of(lax.div(c, per) * HEAD, HEAD), HEAD)
+        return ref.at[rows, cols]
+
+    def remote(src, dst, c, send, recv, to):
+        return pltpu.make_async_remote_copy(
+            src_ref=part(src, c), dst_ref=part(dst, c),
+            send_sem=send, recv_sem=recv,
+            device_id={"ctx": to}, device_id_type=MESH,
+        )
+
+    def z_copy(c):
+        return [
+            remote(src, dst, c, z_send.at[w, c], z_recv.at[w, c], prev2)
+            for w, (src, dst) in enumerate(((q_ref, r2q), (g_ref, r2g)))
+        ]
+
+    def y_copy(c, sources):
+        return [
+            remote(src, dst, c, y_send.at[w, c], y_recv.at[w, c], partner)
+            for w, (src, dst) in enumerate(zip(sources, (r1q, r1g)))
+        ]
+
+    def d1_copy(c):
+        return remote(dq1, rq1, c, d1_send.at[c], d1_recv.at[c], next1)
+
+    def d2_copy(c):
+        return remote(dq2, rq2, c, d2_send.at[c], d2_recv.at[c], next2)
+
+    barrier = pltpu.get_barrier_semaphore()
+    for near, to in ((back1, prev1), (back2, prev2), (has1, next1), (has2, next2)):
+        @pl.when(near)
+        def _():
+            pl.semaphore_signal(barrier, inc=1, device_id={"ctx": to}, device_id_type=MESH)
+    pl.semaphore_wait(barrier, jnp.minimum(p, 2) + jnp.minimum(n - 1 - p, 2))
+
+    def first_sends(c, carry):
+        @pl.when(back2)
+        def _():
+            for copy in z_copy(c):
+                copy.start()
+
+        @pl.when(odd)
+        def _():
+            for copy in y_copy(c, (q_ref, g_ref)):
+                copy.start()
+        return carry
+
+    lax.fori_loop(0, chunks, first_sends, 0)
+
+    row = lax.broadcasted_iota(jnp.int32, (BLK, HEAD), 0)
+    for j in range(per):
+        key_id = p * per + j
+        kept = row < BLK - counts_ref[key_id]
+        for d in range(3):
+            for i in range(per):
+                if (d == 0 and j >= i) or (d == 2 and j < i):
+                    continue
+                query_id = jnp.minimum((p + d) * per + i, total - 1)
+                listed = jnp.int32(0)
+                for slot in range(1, KPB):
+                    listed = jnp.where(blocks_ref[query_id, slot] == key_id, 1, listed)
+                mask[d * per + i, pl.ds(j * BLK, BLK), :] = jnp.where(
+                    kept, listed.astype(jnp.float32), 0.0
+                ).astype(jnp.bfloat16)
+
+    key_row = lax.broadcasted_iota(jnp.int32, (BLK, BLK), 0)
+    query_col = lax.broadcasted_iota(jnp.int32, (BLK, BLK), 1)
+
+    def per_head(h, carry):
+        cols = pl.ds(pl.multiple_of(h * HEAD, HEAD), HEAD)
+        dk_acc[...] = jnp.zeros_like(dk_acc)
+        dv_acc[...] = jnp.zeros_like(dv_acc)
+
+        def source(d, i, query_ref, grad_ref):
+            rows = pl.ds(i * BLK, BLK)
+            query, grad = query_ref[rows, cols], grad_ref[rows, cols]
+            query_sum = None
+            key_slots = {0: range(0, i + 1), 1: range(per), 2: range(i, per)}[d]
+            for j in key_slots:
+                at = pl.ds(j * BLK, BLK)
+                key, value, allowed = k_ref[at, cols], v_ref[at, cols], None
+                if d == 0 and j == i:
+                    limit = BLK - counts_ref[p * per + i]
+                    allowed = (key_row <= query_col) & (
+                        (key_row < limit) | (key_row == query_col)
+                    )
+                else:
+                    read = mask[d * per + i, at, :]
+                    key, value = key * read, value * read
+                query_part, key_part, value_part = tile(query, grad, key, value, allowed)
+                query_sum = query_part if query_sum is None else query_sum + query_part
+                dk_acc[at, :] += key_part
+                dv_acc[at, :] += value_part
+            return query_sum * dq_scale
+
+        for i in range(per):
+            c = h * per + i
+            rows = pl.ds(i * BLK, BLK)
+
+            @pl.when(has2)
+            def _():
+                for copy in z_copy(c):
+                    copy.wait_recv()
+
+                @pl.when(even)
+                def _():
+                    for copy in y_copy(c, (r2q, r2g)):
+                        copy.start()
+
+            dq0[rows, cols] = source(0, i, q_ref, g_ref)
+
+            @pl.when(has2)
+            def _():
+                dq2[rows, cols] = source(2, i, r2q, r2g).astype(jnp.bfloat16)
+                d2_copy(c).start()
+
+            @pl.when(has1)
+            def _():
+                for copy in y_copy(c, (q_ref, g_ref)):
+                    copy.wait_recv()
+                dq1[rows, cols] = source(1, i, r1q, r1g).astype(jnp.bfloat16)
+                d1_copy(c).start()
+
+        dk_ref[:, cols] = (dk_acc[...] * dq_scale).astype(jnp.bfloat16)
+        dv_ref[:, cols] = (dv_acc[...] * NORM_SCALE).astype(jnp.bfloat16)
+        return carry
+
+    lax.fori_loop(0, heads, per_head, 0)
+
+    def finish(c, carry):
+        rows = pl.ds(pl.multiple_of(lax.rem(c, per) * BLK, BLK), BLK)
+        cols = pl.ds(pl.multiple_of(lax.div(c, per) * HEAD, HEAD), HEAD)
+
+        @pl.when(back2)
+        def _():
+            d2_copy(c).wait_recv()
+            dq0[rows, cols] += rq2[rows, cols].astype(jnp.float32)
+            for copy in z_copy(c):
+                copy.wait_send()
+
+        @pl.when(back1)
+        def _():
+            d1_copy(c).wait_recv()
+            dq0[rows, cols] += rq1[rows, cols].astype(jnp.float32)
+
+        dq_ref[rows, cols] = dq0[rows, cols].astype(jnp.bfloat16)
+
+        @pl.when(odd | has2)
+        def _():
+            for copy in y_copy(c, (q_ref, g_ref)):
+                copy.wait_send()
+
+        @pl.when(has1)
+        def _():
+            d1_copy(c).wait_send()
+
+        @pl.when(has2)
+        def _():
+            d2_copy(c).wait_send()
+        return carry
+
+    lax.fori_loop(0, chunks, finish, 0)
+
+
+def near_body(n, queries, keys, values, out_grad, key_blocks, target_counts):
+    rows, columns = queries.shape
+    per, heads = rows // BLK, columns // HEAD
+    chunks = heads * per
+    narrow = pltpu.VMEM((rows, columns), jnp.bfloat16)
+    wide = pltpu.VMEM((rows, columns), jnp.float32)
+    acc = pltpu.VMEM((rows, HEAD), jnp.float32)
+    pair = pltpu.SemaphoreType.DMA((2, chunks))
+    single = pltpu.SemaphoreType.DMA((chunks,))
+    whole = pl.BlockSpec(memory_space=pltpu.VMEM)
+    scalars = pl.BlockSpec(memory_space=pltpu.SMEM)
+    result = jax.ShapeDtypeStruct((rows, columns), jnp.bfloat16)
+    return pl.pallas_call(
+        functools.partial(kernel, n, per, heads),
+        out_shape=(result, result, result),
+        in_specs=[scalars, scalars] + [whole] * 4,
+        out_specs=(whole, whole, whole),
+        scratch_shapes=[narrow] * 8
+        + [wide, acc, acc, pltpu.VMEM((3 * per, rows, HEAD), jnp.bfloat16)]
+        + [pair] * 4 + [single] * 4,
+        compiler_params=pltpu.CompilerParams(
+            collective_id=0, has_side_effects=True, vmem_limit_bytes=48 * 1024 * 1024
+        ),
+    )(key_blocks, target_counts, queries, out_grad, keys, values)
 
 
 def from_behind(array, axis, by):
@@ -170,4 +411,8 @@
 def solution(mesh):
     in_specs = (P("ctx", "tp"), P("ctx", "tp"), P("ctx", "tp"), P("ctx", "tp"), P(), P())
     out_specs = (P("ctx", "tp"), P("ctx", "tp"), P("ctx", "tp"))
-    return jax.shard_map(body, mesh=mesh, in_specs=in_specs, out_specs=out_specs, check_vma=False)
+    length = mesh.shape["ctx"]
+    mapped = functools.partial(near_body, length) if length // 4 == 2 else body
+    return jax.shard_map(
+        mapped, mesh=mesh, in_specs=in_specs, out_specs=out_specs, check_vma=False
+    )

time: 434 us -> 73.7 us (0.17); the launches traced: 427 us -> 73.3 us
  waiting for transfers between devices: 133 us -> 0 us
  matrix products: 120 us -> 0 us
  Pallas kernels: 0 us -> 64.7 us
  local copies, waits for them, and re-layouts: 72.5 us -> 7.95 us
  loops' own time: 45.4 us -> 0 us
  other arithmetic: 36.7 us -> 0 us
  starting transfers between devices: 18 us -> 0 us
    ppermute x7 -> x0, waiting for transfers between devices: 133 us -> none  [the longest x3 71.7 us: passed_along(): lax.ppermute(array, axis, [(i, (i + by) % length) for i in range(length)])]
    dot_general x105 -> x0, matrix products: 120 us -> none  [the longest x21 34 us: tile_grads(): jnp.einsum('ihd,jhd->hij', grad_tile, value_tile, preferred_element_type=...]
    pallas_call x0 -> x1, Pallas kernels: none -> 64.7 us  [near_body(): pl.pallas_call(functools.partial(kernel, n, per, heads), out_shape=(resul...]
    another operation x31 -> x0, loops' own time: 45.4 us -> none  [the longest x27 28.4 us: pair_step(): return lax.cond(listed, work, lambda unchanged: unchanged, present_value)]
    cond x240 -> x0, local copies, waits for them, and re-layouts: 36.4 us -> none
    reduce_or x27 -> x0, other arithmetic: 19.2 us -> none  [pair_step(): listed = active & jnp.any(key_blocks[query_id] == key_id)]
    ppermute x7 -> x0, starting transfers between devices: 18 us -> none  [the longest x4 12.7 us: from_behind(): return lax.ppermute(array, axis, pairs)]
    another operation x21 -> x0, other arithmetic: 15.2 us -> none
  transfers between devices with their start and end apart: 7 -> 0, of which waited for: 7 -> 0; matrix products, arithmetic and copies ran while one was open for 1% -> 0% of each run, Pallas kernels for 0% -> 0%
where the time goes in v1:
time: 73.7 us; the launch traced here: 73.3 us
  Pallas kernels  64.7 us (88%)
  local copies, waits for them, and re-layouts  7.95 us (11%)
    pallas_call x1, Pallas kernels, near_body(): pl.pallas_call(functools.partial(kernel, n, per, heads), out_shape=(resul...  64.7 us
    unnamed x14, local copies, waits for them, and re-layouts  7.95 us

profile of v1, /device:TPU:10, one launch (start us, length us, event | category | flops | bytes accessed | tf_op | source)
XLA Modules:
  0.0 73.3 jit_solution(13511948440696642189)
XLA Ops:
  0.6 0.0 copy-start.4
  0.6 0.8 %copy.9.blocks_ref = s32[24,16]{1,0:T(8,128)S(1)} copy(s32[24,16]{0,1:T(8,128)} %param.10) | data formatting | bytes 3072 | tf_op args[4]
  1.4 0.0 copy-done.4
  1.4 0.0 copy-start
  1.4 1.1 %copy-done = bf16[768,512]{1,0:T(8,128)(2,1)S(1)} copy-done((bf16[768,512]{1,0:T(8,128)(2,1)S(1)}, bf16[768,512]{1,0:T(8,128)(2,1)}, u32[]{:S(2)}) %copy-start) | copy-done | bytes 786456
  2.6 0.0 copy-start.1
  2.6 1.1 %copy-done.1 = bf16[768,512]{1,0:T(8,128)(2,1)S(1)} copy-done((bf16[768,512]{1,0:T(8,128)(2,1)S(1)}, bf16[768,512]{1,0:T(8,128)(2,1)}, u32[]{:S(2)}) %copy-start.1) | copy-done | bytes 786456
  3.7 0.0 copy-start.2
  3.7 1.1 %copy-done.2 = bf16[768,512]{1,0:T(8,128)(2,1)S(1)} copy-done((bf16[768,512]{1,0:T(8,128)(2,1)S(1)}, bf16[768,512]{1,0:T(8,128)(2,1)}, u32[]{:S(2)}) %copy-start.2) | copy-done | bytes 786456
  4.8 0.0 copy-start.3
  4.8 1.1 %copy-done.3 = bf16[768,512]{1,0:T(8,128)(2,1)S(1)} copy-done((bf16[768,512]{1,0:T(8,128)(2,1)S(1)}, bf16[768,512]{1,0:T(8,128)(2,1)}, u32[]{:S(2)}) %copy-start.3) | copy-done | bytes 786456
  6.0 64.7 %shard_map.85 = (bf16[768,512]{1,0:T(8,128)(2,1)S(1)}, bf16[768,512]{1,0:T(8,128)(2,1)S(1)}, bf16[768,512]{1,0:T(8,128)(2,1)S(1)}) custom-call(s32[24,16]{1,0:T(8,128)S(1)} %copy.9.blocks_ref, s32[24]{0:T(128)S(1)} %copy-done.4, bf16[768,512]{1,0:T(8,128)(2,1)S(1)} %copy-done, bf16[768,512]{1,0:T(8,128)(2,1)S(1)} %copy-done.1, ...), custom_call_target="tpu_custom_call" | custom-call | tf_op jit(solution)/shard_map/pallas_call | solution.py:240
  70.7 0.9 %copy.13 = bf16[768,512]{1,0:T(8,128)(2,1)} copy(bf16[768,512]{1,0:T(8,128)(2,1)S(1)} %get-tuple-element.6) | data formatting | bytes 1572864
  71.6 0.9 %copy.14 = bf16[768,512]{1,0:T(8,128)(2,1)} copy(bf16[768,512]{1,0:T(8,128)(2,1)S(1)} %get-tuple-element.7) | data formatting | bytes 1572864
  72.5 0.9 %copy.15 = bf16[768,512]{1,0:T(8,128)(2,1)} copy(bf16[768,512]{1,0:T(8,128)(2,1)S(1)} %get-tuple-element.8) | data formatting | bytes 1572864
Async XLA Ops:
  0.6 0.8 %copy-start.4 = (s32[24]{0:T(128)S(1)}, s32[24]{0:T(128)}, u32[]{:S(2)}) copy-start(s32[24]{0:T(128)} %counts_ref.1) | copy-start | bytes 292
  1.4 1.1 %copy-start = (bf16[768,512]{1,0:T(8,128)(2,1)S(1)}, bf16[768,512]{1,0:T(8,128)(2,1)}, u32[]{:S(2)}) copy-start(bf16[768,512]{1,0:T(8,128)(2,1)} %q_ref.1) | copy-start | bytes 2359300
  2.6 1.1 %copy-start.1 = (bf16[768,512]{1,0:T(8,128)(2,1)S(1)}, bf16[768,512]{1,0:T(8,128)(2,1)}, u32[]{:S(2)}) copy-start(bf16[768,512]{1,0:T(8,128)(2,1)} %g_ref.1) | copy-start | bytes 2359300
  3.7 1.1 %copy-start.2 = (bf16[768,512]{1,0:T(8,128)(2,1)S(1)}, bf16[768,512]{1,0:T(8,128)(2,1)}, u32[]{:S(2)}) copy-start(bf16[768,512]{1,0:T(8,128)(2,1)} %k_ref.1) | copy-start | bytes 2359300
  4.8 1.1 %copy-start.3 = (bf16[768,512]{1,0:T(8,128)(2,1)S(1)}, bf16[768,512]{1,0:T(8,128)(2,1)}, u32[]{:S(2)}) copy-start(bf16[768,512]{1,0:T(8,128)(2,1)} %v_ref.1) | copy-start | bytes 2359300

commit v2 on v1

--- a/solution.py
+++ b/solution.py
@@ -42,10 +42,10 @@
 
 def kernel(
     n, per, heads,
-    blocks_ref, counts_ref, q_ref, g_ref, k_ref, v_ref,
-    dq_ref, dk_ref, dv_ref,
-    r1q, r1g, r2q, r2g, dq1, dq2, rq1, rq2, dq0, dk_acc, dv_acc, mask,
-    z_send, z_recv, y_send, y_recv, d1_send, d1_recv, d2_send, d2_recv,
+    blocks_ref, counts_ref, q_hbm, g_hbm, k_hbm, v_hbm,
+    dq_hbm, dk_hbm, dv_hbm,
+    dq_ref, dk_ref, dv_ref, q_ref, g_ref, k_ref, v_ref, r1q, r1g, r2q, r2g, dq1, dq2, rq1, rq2, dq0, dk_acc, dv_acc, mask,
+    z_send, z_recv, y_send, y_recv, d1_send, d1_recv, d2_send, d2_recv, own, dq_out, dkv_out,
 ):
     p = lax.axis_index("ctx")
     total = n * per
@@ -71,10 +71,20 @@
             device_id={"ctx": to}, device_id_type=MESH,
         )
 
+    def dq_store(c):
+        return pltpu.make_async_copy(part(dq_ref, c), part(dq_hbm, c), dq_out.at[c])
+
+    def dkv_store(h):
+        cols = pl.ds(pl.multiple_of(h * HEAD, HEAD), HEAD)
+        return [
+            pltpu.make_async_copy(src.at[:, cols], dst.at[:, cols], dkv_out.at[w, h])
+            for w, (src, dst) in enumerate(((dk_ref, dk_hbm), (dv_ref, dv_hbm)))
+        ]
+
     def z_copy(c):
         return [
             remote(src, dst, c, z_send.at[w, c], z_recv.at[w, c], prev2)
-            for w, (src, dst) in enumerate(((q_ref, r2q), (g_ref, r2g)))
+            for w, (src, dst) in enumerate(((q_hbm, r2q), (g_hbm, r2g)))
         ]
 
     def y_copy(c, sources):
@@ -89,6 +99,13 @@
     def d2_copy(c):
         return remote(dq2, rq2, c, d2_send.at[c], d2_recv.at[c], next2)
 
+    loads = [
+        pltpu.make_async_copy(src, dst, own.at[w])
+        for w, (src, dst) in enumerate(
+            ((k_hbm, k_ref), (v_hbm, v_ref), (q_hbm, q_ref), (g_hbm, g_ref))
+        )
+    ]
+
     barrier = pltpu.get_barrier_semaphore()
     for near, to in ((back1, prev1), (back2, prev2), (has1, next1), (has2, next2)):
         @pl.when(near)
@@ -104,11 +121,13 @@
 
         @pl.when(odd)
         def _():
-            for copy in y_copy(c, (q_ref, g_ref)):
+            for copy in y_copy(c, (q_hbm, g_hbm)):
                 copy.start()
         return carry
 
     lax.fori_loop(0, chunks, first_sends, 0)
+    for load in loads:
+        load.start()
 
     row = lax.broadcasted_iota(jnp.int32, (BLK, HEAD), 0)
     for j in range(per):
@@ -121,13 +140,17 @@
                 query_id = jnp.minimum((p + d) * per + i, total - 1)
                 listed = jnp.int32(0)
                 for slot in range(1, KPB):
-                    listed = jnp.where(blocks_ref[query_id, slot] == key_id, 1, listed)
+                    listed = jnp.where(blocks_ref[slot, query_id] == key_id, 1, listed)
                 mask[d * per + i, pl.ds(j * BLK, BLK), :] = jnp.where(
                     kept, listed.astype(jnp.float32), 0.0
                 ).astype(jnp.bfloat16)
 
     key_row = lax.broadcasted_iota(jnp.int32, (BLK, BLK), 0)
     query_col = lax.broadcasted_iota(jnp.int32, (BLK, BLK), 1)
+
+    for load in loads:
+        load.wait()
+    late = even & has2
 
     def per_head(h, carry):
         cols = pl.ds(pl.multiple_of(h * HEAD, HEAD), HEAD)
@@ -179,16 +202,29 @@
 
             @pl.when(has1)
             def _():
-                for copy in y_copy(c, (q_ref, g_ref)):
+                for copy in y_copy(c, (q_hbm, g_hbm)):
                     copy.wait_recv()
                 dq1[rows, cols] = source(1, i, r1q, r1g).astype(jnp.bfloat16)
-                d1_copy(c).start()
+
+                @pl.when(jnp.logical_not(late))
+                def _():
+                    d1_copy(c).start()
 
         dk_ref[:, cols] = (dk_acc[...] * dq_scale).astype(jnp.bfloat16)
         dv_ref[:, cols] = (dv_acc[...] * NORM_SCALE).astype(jnp.bfloat16)
+        for store in dkv_store(h):
+            store.start()
         return carry
 
     lax.fori_loop(0, heads, per_head, 0)
+
+    def late_sends(c, carry):
+        d1_copy(c).start()
+        return carry
+
+    @pl.when(late)
+    def _():
+        lax.fori_loop(0, chunks, late_sends, 0)
 
     def finish(c, carry):
         rows = pl.ds(pl.multiple_of(lax.rem(c, per) * BLK, BLK), BLK)
@@ -207,10 +243,11 @@
             dq0[rows, cols] += rq1[rows, cols].astype(jnp.float32)
 
         dq_ref[rows, cols] = dq0[rows, cols].astype(jnp.bfloat16)
+        dq_store(c).start()
 
         @pl.when(odd | has2)
         def _():
-            for copy in y_copy(c, (q_ref, g_ref)):
+            for copy in y_copy(c, (q_hbm, g_hbm)):
                 copy.wait_send()
 
         @pl.when(has1)
@@ -223,6 +260,26 @@
         return carry
 
     lax.fori_loop(0, chunks, finish, 0)
+
+    def stored(h, carry):
+        for store in dkv_store(h):
+            store.wait()
+        for i in range(per):
+            dq_store(h * per + i).wait()
+        return carry
+
+    lax.fori_loop(0, heads, stored, 0)
+
+
+def hand_over(a_in, b_in, c_in, a_out, b_out, c_out, done):
+    copies = [
+        pltpu.make_async_copy(src, dst, done.at[w])
+        for w, (src, dst) in enumerate(((a_in, a_out), (b_in, b_out), (c_in, c_out)))
+    ]
+    for copy in copies:
+        copy.start()
+    for copy in copies:
+        copy.wait()
 
 
 def near_body(n, queries, keys, values, out_grad, key_blocks, target_counts):
@@ -234,21 +291,28 @@
     acc = pltpu.VMEM((rows, HEAD), jnp.float32)
     pair = pltpu.SemaphoreType.DMA((2, chunks))
     single = pltpu.SemaphoreType.DMA((chunks,))
-    whole = pl.BlockSpec(memory_space=pltpu.VMEM)
     scalars = pl.BlockSpec(memory_space=pltpu.SMEM)
     result = jax.ShapeDtypeStruct((rows, columns), jnp.bfloat16)
-    return pl.pallas_call(
+    grads = pl.pallas_call(
         functools.partial(kernel, n, per, heads),
         out_shape=(result, result, result),
-        in_specs=[scalars, scalars] + [whole] * 4,
-        out_specs=(whole, whole, whole),
-        scratch_shapes=[narrow] * 8
+        in_specs=[scalars, scalars] + [pl.BlockSpec(memory_space=pl.ANY)] * 4,
+        out_specs=(pl.BlockSpec(memory_space=pl.ANY),) * 3,
+        scratch_shapes=[narrow] * 15
         + [wide, acc, acc, pltpu.VMEM((3 * per, rows, HEAD), jnp.bfloat16)]
-        + [pair] * 4 + [single] * 4,
+        + [pair] * 4 + [single] * 4 + [pltpu.SemaphoreType.DMA((4,)), single, pltpu.SemaphoreType.DMA((2, heads))],
         compiler_params=pltpu.CompilerParams(
-            collective_id=0, has_side_effects=True, vmem_limit_bytes=48 * 1024 * 1024
+            collective_id=0, has_side_effects=True, vmem_limit_bytes=56 * 1024 * 1024
         ),
-    )(key_blocks, target_counts, queries, out_grad, keys, values)
+    )(key_blocks.T, target_counts, queries, out_grad, keys, values)
+    return pl.pallas_call(
+        hand_over,
+        out_shape=(result, result, result),
+        in_specs=[pl.BlockSpec(memory_space=pl.ANY)] * 3,
+        out_specs=(pl.BlockSpec(memory_space=pl.ANY),) * 3,
+        scratch_shapes=[pltpu.SemaphoreType.DMA((3,))],
+        compiler_params=pltpu.CompilerParams(vmem_limit_bytes=56 * 1024 * 1024),
+    )(*grads)
 
 
 def from_behind(array, axis, by):

time: 73.7 us -> 151 us (2.05); the launches traced: 73.3 us -> 149 us
  Pallas kernels: 64.7 us -> 148 us
  local copies, waits for them, and re-layouts: 7.95 us -> 0 us
    pallas_call x0 -> x1, Pallas kernels: none -> 72.6 us  [near_body(): pl.pallas_call(hand_over, out_shape=(result, result, result), in_specs=[p...]
    pallas_call x1, Pallas kernels: 64.7 us -> 75.5 us  [near_body(): pl.pallas_call(functools.partial(kernel, n, per, heads), out_shape=(resul...]
    unnamed x14 -> x0, local copies, waits for them, and re-layouts: 7.95 us -> none
where the time goes in v2:
time: 151 us; the launch traced here: 149 us
  Pallas kernels  148 us (98%)
    pallas_call x1, Pallas kernels, near_body(): pl.pallas_call(functools.partial(kernel, n, per, heads), out_shape=(resul...  75.5 us
    pallas_call x1, Pallas kernels, near_body(): pl.pallas_call(hand_over, out_shape=(result, result, result), in_specs=[p...  72.6 us

profile of v2, /device:TPU:10, one launch (start us, length us, event | category | flops | bytes accessed | tf_op | source)
XLA Modules:
  0.0 148.7 jit_solution(3620636632701413933)
XLA Ops:
  0.6 75.5 %shard_map.85 = (bf16[768,512]{1,0:T(8,128)(2,1)}, bf16[768,512]{1,0:T(8,128)(2,1)}, bf16[768,512]{1,0:T(8,128)(2,1)}) custom-call(s32[16,24]{1,0:T(8,128)} %bitcast.1, s32[24]{0:T(128)} %counts_ref.1, bf16[768,512]{1,0:T(8,128)(2,1)} %q_hbm.1, bf16[768,512]{1,0:T(8,128)(2,1)} %g_hbm.1, bf16[768,512]{1,0:T(8,128)(2,1)} %k_hbm.1, bf16[768,512]{1,0:T(8,128)(2,1)} %v_hbm.1), custom_call_target="tpu_custom_call" | custom-call | tf_op jit(solution)/shard_map/pallas_call | solution.py:296
  76.1 72.6 %shard_map.86 = (bf16[768,512]{1,0:T(8,128)(2,1)}, bf16[768,512]{1,0:T(8,128)(2,1)}, bf16[768,512]{1,0:T(8,128)(2,1)}) custom-call(bf16[768,512]{1,0:T(8,128)(2,1)} %get-tuple-element.6.a_in, bf16[768,512]{1,0:T(8,128)(2,1)} %get-tuple-element.7.b_in, bf16[768,512]{1,0:T(8,128)(2,1)} %get-tuple-element.8.c_in), custom_call_target="tpu_custom_call" | custom-call | tf_op jit(solution)/shard_map/pallas_call | solution.py:308

commit v3 on v2

--- a/solution.py
+++ b/solution.py
@@ -84,7 +84,7 @@
     def z_copy(c):
         return [
             remote(src, dst, c, z_send.at[w, c], z_recv.at[w, c], prev2)
-            for w, (src, dst) in enumerate(((q_hbm, r2q), (g_hbm, r2g)))
+            for w, (src, dst) in enumerate(((q_ref, r2q), (g_ref, r2g)))
         ]
 
     def y_copy(c, sources):
@@ -102,9 +102,12 @@
     loads = [
         pltpu.make_async_copy(src, dst, own.at[w])
         for w, (src, dst) in enumerate(
-            ((k_hbm, k_ref), (v_hbm, v_ref), (q_hbm, q_ref), (g_hbm, g_ref))
+            ((q_hbm, q_ref), (g_hbm, g_ref), (k_hbm, k_ref), (v_hbm, v_ref))
         )
     ]
+
+    for load in loads:
+        load.start()
 
     barrier = pltpu.get_barrier_semaphore()
     for near, to in ((back1, prev1), (back2, prev2), (has1, next1), (has2, next2)):
@@ -121,13 +124,13 @@
 
         @pl.when(odd)
         def _():
-            for copy in y_copy(c, (q_hbm, g_hbm)):
+            for copy in y_copy(c, (q_ref, g_ref)):
                 copy.start()
         return carry
 
+    for load in loads[:2]:
+        load.wait()
     lax.fori_loop(0, chunks, first_sends, 0)
-    for load in loads:
-        load.start()
 
     row = lax.broadcasted_iota(jnp.int32, (BLK, HEAD), 0)
     for j in range(per):
@@ -148,83 +151,88 @@
     key_row = lax.broadcasted_iota(jnp.int32, (BLK, BLK), 0)
     query_col = lax.broadcasted_iota(jnp.int32, (BLK, BLK), 1)
 
-    for load in loads:
+    dk_acc[...] = jnp.zeros_like(dk_acc)
+    dv_acc[...] = jnp.zeros_like(dv_acc)
+    for load in loads[2:]:
         load.wait()
-    late = even & has2
-
-    def per_head(h, carry):
+
+    def source(d, h, i, query_ref, grad_ref):
+        rows = pl.ds(i * BLK, BLK)
         cols = pl.ds(pl.multiple_of(h * HEAD, HEAD), HEAD)
-        dk_acc[...] = jnp.zeros_like(dk_acc)
-        dv_acc[...] = jnp.zeros_like(dv_acc)
-
-        def source(d, i, query_ref, grad_ref):
+        query, grad = query_ref[rows, cols], grad_ref[rows, cols]
+        query_sum = None
+        key_slots = {0: range(0, i + 1), 1: range(per), 2: range(i, per)}[d]
+        for j in key_slots:
+            at = pl.ds(j * BLK, BLK)
+            key, value, allowed = k_ref[at, cols], v_ref[at, cols], None
+            if d == 0 and j == i:
+                limit = BLK - counts_ref[p * per + i]
+                allowed = (key_row <= query_col) & (
+                    (key_row < limit) | (key_row == query_col)
+                )
+            else:
+                read = mask[d * per + i, at, :]
+                key, value = key * read, value * read
+            query_part, key_part, value_part = tile(query, grad, key, value, allowed)
+            query_sum = query_part if query_sum is None else query_sum + query_part
+            dk_acc[at, cols] += key_part
+            dv_acc[at, cols] += value_part
+        return query_sum * dq_scale
+
+    def returns(c, carry):
+        d1_copy(c).start()
+        return carry
+
+    def one_round(h, carry):
+        @pl.when((h == heads) & has1)
+        def _():
+            lax.fori_loop(0, chunks - per, returns, 0)
+
+        for i in range(per):
             rows = pl.ds(i * BLK, BLK)
-            query, grad = query_ref[rows, cols], grad_ref[rows, cols]
-            query_sum = None
-            key_slots = {0: range(0, i + 1), 1: range(per), 2: range(i, per)}[d]
-            for j in key_slots:
-                at = pl.ds(j * BLK, BLK)
-                key, value, allowed = k_ref[at, cols], v_ref[at, cols], None
-                if d == 0 and j == i:
-                    limit = BLK - counts_ref[p * per + i]
-                    allowed = (key_row <= query_col) & (
-                        (key_row < limit) | (key_row == query_col)
-                    )
-                else:
-                    read = mask[d * per + i, at, :]
-                    key, value = key * read, value * read
-                query_part, key_part, value_part = tile(query, grad, key, value, allowed)
-                query_sum = query_part if query_sum is None else query_sum + query_part
-                dk_acc[at, :] += key_part
-                dv_acc[at, :] += value_part
-            return query_sum * dq_scale
-
-        for i in range(per):
-            c = h * per + i
-            rows = pl.ds(i * BLK, BLK)
-
-            @pl.when(has2)
+
+            @pl.when(h < heads)
             def _():
-                for copy in z_copy(c):
+                c = h * per + i
+                cols = pl.ds(pl.multiple_of(h * HEAD, HEAD), HEAD)
+
+                @pl.when(has2)
+                def _():
+                    for copy in z_copy(c):
+                        copy.wait_recv()
+
+                    @pl.when(even)
+                    def _():
+                        for copy in y_copy(c, (r2q, r2g)):
+                            copy.start()
+
+                    dq2[rows, cols] = source(2, h, i, r2q, r2g).astype(jnp.bfloat16)
+                    d2_copy(c).start()
+
+                dq0[rows, cols] = source(0, h, i, q_ref, g_ref)
+
+            @pl.when((h > 0) & has1)
+            def _():
+                c = (h - 1) * per + i
+                cols = pl.ds(pl.multiple_of((h - 1) * HEAD, HEAD), HEAD)
+                for copy in y_copy(c, (q_ref, g_ref)):
                     copy.wait_recv()
-
-                @pl.when(even)
-                def _():
-                    for copy in y_copy(c, (r2q, r2g)):
-                        copy.start()
-
-            dq0[rows, cols] = source(0, i, q_ref, g_ref)
-
-            @pl.when(has2)
-            def _():
-                dq2[rows, cols] = source(2, i, r2q, r2g).astype(jnp.bfloat16)
-                d2_copy(c).start()
-
-            @pl.when(has1)
-            def _():
-                for copy in y_copy(c, (q_hbm, g_hbm)):
-                    copy.wait_recv()
-                dq1[rows, cols] = source(1, i, r1q, r1g).astype(jnp.bfloat16)
-
-                @pl.when(jnp.logical_not(late))
+                dq1[rows, cols] = source(1, h - 1, i, r1q, r1g).astype(jnp.bfloat16)
+
+                @pl.when(h == heads)
                 def _():
                     d1_copy(c).start()
 
-        dk_ref[:, cols] = (dk_acc[...] * dq_scale).astype(jnp.bfloat16)
-        dv_ref[:, cols] = (dv_acc[...] * NORM_SCALE).astype(jnp.bfloat16)
-        for store in dkv_store(h):
-            store.start()
+        @pl.when(h > 0)
+        def _():
+            cols = pl.ds(pl.multiple_of((h - 1) * HEAD, HEAD), HEAD)
+            dk_ref[:, cols] = (dk_acc[:, cols] * dq_scale).astype(jnp.bfloat16)
+            dv_ref[:, cols] = (dv_acc[:, cols] * NORM_SCALE).astype(jnp.bfloat16)
+            for store in dkv_store(h - 1):
+                store.start()
         return carry
 
-    lax.fori_loop(0, heads, per_head, 0)
-
-    def late_sends(c, carry):
-        d1_copy(c).start()
-        return carry
-
-    @pl.when(late)
-    def _():
-        lax.fori_loop(0, chunks, late_sends, 0)
+    lax.fori_loop(0, heads + 1, one_round, 0)
 
     def finish(c, carry):
         rows = pl.ds(pl.multiple_of(lax.rem(c, per) * BLK, BLK), BLK)
@@ -247,7 +255,7 @@
 
         @pl.when(odd | has2)
         def _():
-            for copy in y_copy(c, (q_hbm, g_hbm)):
+            for copy in y_copy(c, (q_ref, g_ref)):
                 copy.wait_send()
 
         @pl.when(has1)
@@ -271,48 +279,29 @@
     lax.fori_loop(0, heads, stored, 0)
 
 
-def hand_over(a_in, b_in, c_in, a_out, b_out, c_out, done):
-    copies = [
-        pltpu.make_async_copy(src, dst, done.at[w])
-        for w, (src, dst) in enumerate(((a_in, a_out), (b_in, b_out), (c_in, c_out)))
-    ]
-    for copy in copies:
-        copy.start()
-    for copy in copies:
-        copy.wait()
-
-
 def near_body(n, queries, keys, values, out_grad, key_blocks, target_counts):
     rows, columns = queries.shape
     per, heads = rows // BLK, columns // HEAD
     chunks = heads * per
     narrow = pltpu.VMEM((rows, columns), jnp.bfloat16)
     wide = pltpu.VMEM((rows, columns), jnp.float32)
-    acc = pltpu.VMEM((rows, HEAD), jnp.float32)
     pair = pltpu.SemaphoreType.DMA((2, chunks))
     single = pltpu.SemaphoreType.DMA((chunks,))
     scalars = pl.BlockSpec(memory_space=pltpu.SMEM)
     result = jax.ShapeDtypeStruct((rows, columns), jnp.bfloat16)
-    grads = pl.pallas_call(
+    return pl.pallas_call(
         functools.partial(kernel, n, per, heads),
         out_shape=(result, result, result),
         in_specs=[scalars, scalars] + [pl.BlockSpec(memory_space=pl.ANY)] * 4,
         out_specs=(pl.BlockSpec(memory_space=pl.ANY),) * 3,
         scratch_shapes=[narrow] * 15
-        + [wide, acc, acc, pltpu.VMEM((3 * per, rows, HEAD), jnp.bfloat16)]
+        + [wide] * 3
+        + [pltpu.VMEM((3 * per, rows, HEAD), jnp.bfloat16)]
         + [pair] * 4 + [single] * 4 + [pltpu.SemaphoreType.DMA((4,)), single, pltpu.SemaphoreType.DMA((2, heads))],
         compiler_params=pltpu.CompilerParams(
             collective_id=0, has_side_effects=True, vmem_limit_bytes=56 * 1024 * 1024
         ),
     )(key_blocks.T, target_counts, queries, out_grad, keys, values)
-    return pl.pallas_call(
-        hand_over,
-        out_shape=(result, result, result),
-        in_specs=[pl.BlockSpec(memory_space=pl.ANY)] * 3,
-        out_specs=(pl.BlockSpec(memory_space=pl.ANY),) * 3,
-        scratch_shapes=[pltpu.SemaphoreType.DMA((3,))],
-        compiler_params=pltpu.CompilerParams(vmem_limit_bytes=56 * 1024 * 1024),
-    )(*grads)
 
 
 def from_behind(array, axis, by):

time: 151 us -> 67.4 us (0.45); the launches traced: 149 us -> 67.1 us
  Pallas kernels: 148 us -> 62 us
  local copies, waits for them, and re-layouts: 0 us -> 4.44 us
    pallas_call x1 -> x0, Pallas kernels: 72.6 us -> none  [near_body(): pl.pallas_call(hand_over, out_shape=(result, result, result), in_specs=[p...]
    pallas_call x1, Pallas kernels: 75.5 us -> 62 us  [near_body(): pl.pallas_call(functools.partial(kernel, n, per, heads), out_shape=(resul...]
    unnamed x0 -> x7, local copies, waits for them, and re-layouts: none -> 4.44 us
where the time goes in v3:
time: 67.4 us; the launch traced here: 67.1 us
  Pallas kernels  62 us (92%)
  local copies, waits for them, and re-layouts  4.44 us (7%)
    pallas_call x1, Pallas kernels, near_body(): pl.pallas_call(functools.partial(kernel, n, per, heads), out_shape=(resul...  62 us
    unnamed x7, local copies, waits for them, and re-layouts  4.44 us

profile of v3, /device:TPU:10, one launch (start us, length us, event | category | flops | bytes accessed | tf_op | source)
XLA Modules:
  0.0 67.1 jit_solution(18293364156194048400)
XLA Ops:
  0.6 62.0 %shard_map.85 = (bf16[768,512]{1,0:T(8,128)(2,1)}, bf16[768,512]{1,0:T(8,128)(2,1)}, bf16[768,512]{1,0:T(8,128)(2,1)}) custom-call(s32[16,24]{1,0:T(8,128)} %bitcast.1, s32[24]{0:T(128)} %counts_ref.1, bf16[768,512]{1,0:T(8,128)(2,1)} %q_hbm.1, bf16[768,512]{1,0:T(8,128)(2,1)} %g_hbm.1, bf16[768,512]{1,0:T(8,128)(2,1)} %k_hbm.1, bf16[768,512]{1,0:T(8,128)(2,1)} %v_hbm.1), custom_call_target="tpu_custom_call" | custom-call | tf_op jit(solution)/shard_map/pallas_call | solution.py:292
  62.7 0.0 copy-start.1
  62.7 2.1 %copy.12 = bf16[768,512]{1,0:T(8,128)(2,1)} copy(bf16[768,512]{1,0:T(8,128)(2,1)} %get-tuple-element.6) | data formatting | bytes 1572864
  64.8 0.0 copy-done.1
  64.8 0.0 copy-start
  64.8 0.9 %copy.13 = bf16[768,512]{1,0:T(8,128)(2,1)} copy(bf16[768,512]{1,0:T(8,128)(2,1)S(1)} %copy-done.1) | data formatting | bytes 1572864
  65.7 0.5 copy-done
  66.2 0.9 %copy.14 = bf16[768,512]{1,0:T(8,128)(2,1)} copy(bf16[768,512]{1,0:T(8,128)(2,1)S(1)} %copy-done) | data formatting | bytes 1572864
Async XLA Ops:
  62.7 2.1 %copy-start.1 = (bf16[768,512]{1,0:T(8,128)(2,1)S(1)}, bf16[768,512]{1,0:T(8,128)(2,1)}, u32[]{:S(2)}) copy-start(bf16[768,512]{1,0:T(8,128)(2,1)} %get-tuple-element.7) | copy-start | bytes 2359300
  64.8 1.4 %copy-start = (bf16[768,512]{1,0:T(8,128)(2,1)S(1)}, bf16[768,512]{1,0:T(8,128)(2,1)}, u32[]{:S(2)}) copy-start(bf16[768,512]{1,0:T(8,128)(2,1)} %get-tuple-element.8) | copy-start | bytes 2359300

commit v4 on v3

--- a/solution.py
+++ b/solution.py
@@ -20,15 +20,11 @@
     return lax.dot_general(a, b, (((1,), (1,)), ((), ())), preferred_element_type=jnp.float32)
 
 
-def tn(a, b):
-    return lax.dot_general(a, b, (((0,), (0,)), ((), ())), preferred_element_type=jnp.float32)
-
-
-def tile(query, grad, key, value, allowed=None):
+def tile(query, grad, key, value, key_columns, allowed=None):
     half = nt(key, query) * (0.5 * HEAD_FACTOR)
     one_tanh = 1.0 + jnp.tanh(half)
     weights = half * one_tanh
-    score_grad = nt(value, grad) * (one_tanh * ((1.0 + (half + half)) - weights))
+    score_grad = nt(value, grad) * (one_tanh + weights * (2.0 - one_tanh))
     if allowed is not None:
         weights = jnp.where(allowed, weights, 0.0)
         score_grad = jnp.where(allowed, score_grad, 0.0)
@@ -36,7 +32,7 @@
     score_grad = score_grad.astype(jnp.bfloat16)
     value_part = jnp.dot(weights, grad, preferred_element_type=jnp.float32)
     key_part = jnp.dot(score_grad, query, preferred_element_type=jnp.float32)
-    query_part = tn(score_grad, key)
+    query_part = jnp.dot(key_columns, score_grad, preferred_element_type=jnp.float32)
     return query_part, key_part, value_part
 
 
@@ -44,7 +40,7 @@
     n, per, heads,
     blocks_ref, counts_ref, q_hbm, g_hbm, k_hbm, v_hbm,
     dq_hbm, dk_hbm, dv_hbm,
-    dq_ref, dk_ref, dv_ref, q_ref, g_ref, k_ref, v_ref, r1q, r1g, r2q, r2g, dq1, dq2, rq1, rq2, dq0, dk_acc, dv_acc, mask,
+    dq_ref, dk_ref, dv_ref, q_ref, g_ref, k_ref, v_ref, kt_ref, r1q, r1g, r2q, r2g, dq1, dq2, rq1, rq2, dq0, dk_acc, dv_acc, mask,
     z_send, z_recv, y_send, y_recv, d1_send, d1_recv, d2_send, d2_recv, own, dq_out, dkv_out,
 ):
     p = lax.axis_index("ctx")
@@ -155,6 +151,9 @@
     dv_acc[...] = jnp.zeros_like(dv_acc)
     for load in loads[2:]:
         load.wait()
+    for h in range(heads):
+        cols = pl.ds(h * HEAD, HEAD)
+        kt_ref[cols, :] = k_ref[:, cols].astype(jnp.float32).T.astype(jnp.bfloat16)
 
     def source(d, h, i, query_ref, grad_ref):
         rows = pl.ds(i * BLK, BLK)
@@ -173,21 +172,15 @@
             else:
                 read = mask[d * per + i, at, :]
                 key, value = key * read, value * read
-            query_part, key_part, value_part = tile(query, grad, key, value, allowed)
+            query_part, key_part, value_part = tile(
+                query, grad, key, value, kt_ref[cols, at], allowed
+            )
             query_sum = query_part if query_sum is None else query_sum + query_part
             dk_acc[at, cols] += key_part
             dv_acc[at, cols] += value_part
-        return query_sum * dq_scale
-
-    def returns(c, carry):
-        d1_copy(c).start()
-        return carry
+        return query_sum.T * dq_scale
 
     def one_round(h, carry):
-        @pl.when((h == heads) & has1)
-        def _():
-            lax.fori_loop(0, chunks - per, returns, 0)
-
         for i in range(per):
             rows = pl.ds(i * BLK, BLK)
 
@@ -218,10 +211,7 @@
                 for copy in y_copy(c, (q_ref, g_ref)):
                     copy.wait_recv()
                 dq1[rows, cols] = source(1, h - 1, i, r1q, r1g).astype(jnp.bfloat16)
-
-                @pl.when(h == heads)
-                def _():
-                    d1_copy(c).start()
+                d1_copy(c).start()
 
         @pl.when(h > 0)
         def _():
@@ -277,6 +267,24 @@
         return carry
 
     lax.fori_loop(0, heads, stored, 0)
+
+
+def hand_over(a_in, b_in, c_in, a_out, b_out, c_out, a, b, c, come, gone):
+    half = a.shape[0] // 2
+    steps = [
+        (src.at[pl.ds(at, half)], held.at[pl.ds(at, half)], dst.at[pl.ds(at, half)])
+        for src, held, dst in ((a_in, a, a_out), (b_in, b, b_out), (c_in, c, c_out))
+        for at in (0, half)
+    ]
+    ins = [pltpu.make_async_copy(x, y, come.at[w]) for w, (x, y, _) in enumerate(steps)]
+    outs = [pltpu.make_async_copy(y, z, gone.at[w]) for w, (_, y, z) in enumerate(steps)]
+    for copy in ins:
+        copy.start()
+    for copy, later in zip(ins, outs):
+        copy.wait()
+        later.start()
+    for copy in outs:
+        copy.wait()
 
 
 def near_body(n, queries, keys, values, out_grad, key_blocks, target_counts):
@@ -289,12 +297,14 @@
     single = pltpu.SemaphoreType.DMA((chunks,))
     scalars = pl.BlockSpec(memory_space=pltpu.SMEM)
     result = jax.ShapeDtypeStruct((rows, columns), jnp.bfloat16)
-    return pl.pallas_call(
+    grads = pl.pallas_call(
         functools.partial(kernel, n, per, heads),
         out_shape=(result, result, result),
         in_specs=[scalars, scalars] + [pl.BlockSpec(memory_space=pl.ANY)] * 4,
         out_specs=(pl.BlockSpec(memory_space=pl.ANY),) * 3,
-        scratch_shapes=[narrow] * 15
+        scratch_shapes=[narrow] * 7
+        + [pltpu.VMEM((columns, rows), jnp.bfloat16)]
+        + [narrow] * 8
         + [wide] * 3
         + [pltpu.VMEM((3 * per, rows, HEAD), jnp.bfloat16)]
         + [pair] * 4 + [single] * 4 + [pltpu.SemaphoreType.DMA((4,)), single, pltpu.SemaphoreType.DMA((2, heads))],
@@ -302,6 +312,14 @@
             collective_id=0, has_side_effects=True, vmem_limit_bytes=56 * 1024 * 1024
         ),
     )(key_blocks.T, target_counts, queries, out_grad, keys, values)
+    return pl.pallas_call(
+        hand_over,
+        out_shape=(result, result, result),
+        in_specs=[pl.BlockSpec(memory_space=pl.ANY)] * 3,
+        out_specs=(pl.BlockSpec(memory_space=pl.ANY),) * 3,
+        scratch_shapes=[narrow] * 3 + [pltpu.SemaphoreType.DMA((6,))] * 2,
+        compiler_params=pltpu.CompilerParams(vmem_limit_bytes=56 * 1024 * 1024),
+    )(*grads)
 
 
 def from_behind(array, axis, by):

time: 67.4 us -> 65.6 us (0.973)
  local copies, waits for them, and re-layouts: 4.44 us -> 0 us
  Pallas kernels: 62 us -> 64.7 us
    unnamed x7 -> x0, local copies, waits for them, and re-layouts: 4.44 us -> none
    pallas_call x0 -> x1, Pallas kernels: none -> 2.49 us  [near_body(): pl.pallas_call(hand_over, out_shape=(result, result, result), in_specs=[p...]
where the time goes in v4:
time: 65.6 us; the launch traced here: 65.4 us
  Pallas kernels  64.7 us (99%)
    pallas_call x1, Pallas kernels, near_body(): pl.pallas_call(functools.partial(kernel, n, per, heads), out_shape=(resul...  62.2 us
    pallas_call x1, Pallas kernels, near_body(): pl.pallas_call(hand_over, out_shape=(result, result, result), in_specs=[p...  2.49 us

profile of v4, /device:TPU:10, one launch (start us, length us, event | category | flops | bytes accessed | tf_op | source)
XLA Modules:
  0.0 65.4 jit_solution(17144387555403559515)
XLA Ops:
  0.6 62.2 %shard_map.85 = (bf16[768,512]{1,0:T(8,128)(2,1)}, bf16[768,512]{1,0:T(8,128)(2,1)}, bf16[768,512]{1,0:T(8,128)(2,1)}) custom-call(s32[16,24]{1,0:T(8,128)} %bitcast.1, s32[24]{0:T(128)} %counts_ref.1, bf16[768,512]{1,0:T(8,128)(2,1)} %q_hbm.1, bf16[768,512]{1,0:T(8,128)(2,1)} %g_hbm.1, bf16[768,512]{1,0:T(8,128)(2,1)} %k_hbm.1, bf16[768,512]{1,0:T(8,128)(2,1)} %v_hbm.1), custom_call_target="tpu_custom_call" | custom-call | tf_op jit(solution)/shard_map/pallas_call | solution.py:300
  62.9 2.5 %shard_map.86 = (bf16[768,512]{1,0:T(8,128)(2,1)}, bf16[768,512]{1,0:T(8,128)(2,1)}, bf16[768,512]{1,0:T(8,128)(2,1)}) custom-call(bf16[768,512]{1,0:T(8,128)(2,1)} %get-tuple-element.6.a_in, bf16[768,512]{1,0:T(8,128)(2,1)} %get-tuple-element.7.b_in, bf16[768,512]{1,0:T(8,128)(2,1)} %get-tuple-element.8.c_in), custom_call_target="tpu_custom_call" | custom-call | tf_op jit(solution)/shard_map/pallas_call | solution.py:315

commit v5 on v4

--- a/solution.py
+++ b/solution.py
@@ -40,8 +40,8 @@
     n, per, heads,
     blocks_ref, counts_ref, q_hbm, g_hbm, k_hbm, v_hbm,
     dq_hbm, dk_hbm, dv_hbm,
-    dq_ref, dk_ref, dv_ref, q_ref, g_ref, k_ref, v_ref, kt_ref, r1q, r1g, r2q, r2g, dq1, dq2, rq1, rq2, dq0, dk_acc, dv_acc, mask,
-    z_send, z_recv, y_send, y_recv, d1_send, d1_recv, d2_send, d2_recv, own, dq_out, dkv_out,
+    dq_ref, dk_ref, dv_ref, qg_ref, k_ref, v_ref, kt_ref, r1, r2, dq1, dq2, rq1, rq2, dq0, dk_acc, dv_acc, mask,
+    z_send, z_recv, y_send, y_recv, d1_send, d1_recv, d2_send, d2_recv, qg_own, kv_own, dq_out, dkv_out,
 ):
     p = lax.axis_index("ctx")
     total = n * per
@@ -60,50 +60,69 @@
         cols = pl.ds(pl.multiple_of(lax.div(c, per) * HEAD, HEAD), HEAD)
         return ref.at[rows, cols]
 
+    def columns(ref, h):
+        return ref.at[:, pl.ds(pl.multiple_of(h * HEAD, HEAD), HEAD)]
+
     def remote(src, dst, c, send, recv, to):
         return pltpu.make_async_remote_copy(
-            src_ref=part(src, c), dst_ref=part(dst, c),
-            send_sem=send, recv_sem=recv,
+            src_ref=src.at[c], dst_ref=dst.at[c],
+            send_sem=send.at[c], recv_sem=recv.at[c],
             device_id={"ctx": to}, device_id_type=MESH,
         )
 
+    def qg_load(c):
+        return [
+            pltpu.make_async_copy(
+                part(src, c), qg_ref.at[c, pl.ds(w * BLK, BLK)], qg_own.at[w, c]
+            )
+            for w, src in enumerate((q_hbm, g_hbm))
+        ]
+
+    def kv_load(h):
+        return [
+            pltpu.make_async_copy(columns(src, h), dst.at[h], kv_own.at[w, h])
+            for w, (src, dst) in enumerate(((k_hbm, k_ref), (v_hbm, v_ref)))
+        ]
+
     def dq_store(c):
-        return pltpu.make_async_copy(part(dq_ref, c), part(dq_hbm, c), dq_out.at[c])
+        return pltpu.make_async_copy(dq_ref.at[c], part(dq_hbm, c), dq_out.at[c])
 
     def dkv_store(h):
-        cols = pl.ds(pl.multiple_of(h * HEAD, HEAD), HEAD)
         return [
-            pltpu.make_async_copy(src.at[:, cols], dst.at[:, cols], dkv_out.at[w, h])
+            pltpu.make_async_copy(src.at[h], columns(dst, h), dkv_out.at[w, h])
             for w, (src, dst) in enumerate(((dk_ref, dk_hbm), (dv_ref, dv_hbm)))
         ]
 
     def z_copy(c):
-        return [
-            remote(src, dst, c, z_send.at[w, c], z_recv.at[w, c], prev2)
-            for w, (src, dst) in enumerate(((q_ref, r2q), (g_ref, r2g)))
-        ]
-
-    def y_copy(c, sources):
-        return [
-            remote(src, dst, c, y_send.at[w, c], y_recv.at[w, c], partner)
-            for w, (src, dst) in enumerate(zip(sources, (r1q, r1g)))
-        ]
+        return remote(qg_ref, r2, c, z_send, z_recv, prev2)
+
+    def y_copy(c, source):
+        return remote(source, r1, c, y_send, y_recv, partner)
 
     def d1_copy(c):
-        return remote(dq1, rq1, c, d1_send.at[c], d1_recv.at[c], next1)
+        return remote(dq1, rq1, c, d1_send, d1_recv, next1)
 
     def d2_copy(c):
-        return remote(dq2, rq2, c, d2_send.at[c], d2_recv.at[c], next2)
-
-    loads = [
-        pltpu.make_async_copy(src, dst, own.at[w])
-        for w, (src, dst) in enumerate(
-            ((q_hbm, q_ref), (g_hbm, g_ref), (k_hbm, k_ref), (v_hbm, v_ref))
-        )
-    ]
-
-    for load in loads:
-        load.start()
+        return remote(dq2, rq2, c, d2_send, d2_recv, next2)
+
+    def start_qg(c, carry):
+        for load in qg_load(c):
+            load.start()
+        return carry
+
+    def start_kv(h, carry):
+        for load in kv_load(h):
+            load.start()
+        return carry
+
+    def wait_kv(h, carry):
+        for load in kv_load(h):
+            load.wait()
+        kt_ref[h] = k_ref[h].astype(jnp.float32).T.astype(jnp.bfloat16)
+        return carry
+
+    lax.fori_loop(0, chunks, start_qg, 0)
+    lax.fori_loop(0, heads, start_kv, 0)
 
     barrier = pltpu.get_barrier_semaphore()
     for near, to in ((back1, prev1), (back2, prev2), (has1, next1), (has2, next2)):
@@ -113,19 +132,18 @@
     pl.semaphore_wait(barrier, jnp.minimum(p, 2) + jnp.minimum(n - 1 - p, 2))
 
     def first_sends(c, carry):
+        for load in qg_load(c):
+            load.wait()
+
         @pl.when(back2)
         def _():
-            for copy in z_copy(c):
-                copy.start()
+            z_copy(c).start()
 
         @pl.when(odd)
         def _():
-            for copy in y_copy(c, (q_ref, g_ref)):
-                copy.start()
-        return carry
-
-    for load in loads[:2]:
-        load.wait()
+            y_copy(c, qg_ref).start()
+        return carry
+
     lax.fori_loop(0, chunks, first_sends, 0)
 
     row = lax.broadcasted_iota(jnp.int32, (BLK, HEAD), 0)
@@ -149,21 +167,16 @@
 
     dk_acc[...] = jnp.zeros_like(dk_acc)
     dv_acc[...] = jnp.zeros_like(dv_acc)
-    for load in loads[2:]:
-        load.wait()
-    for h in range(heads):
-        cols = pl.ds(h * HEAD, HEAD)
-        kt_ref[cols, :] = k_ref[:, cols].astype(jnp.float32).T.astype(jnp.bfloat16)
-
-    def source(d, h, i, query_ref, grad_ref):
-        rows = pl.ds(i * BLK, BLK)
-        cols = pl.ds(pl.multiple_of(h * HEAD, HEAD), HEAD)
-        query, grad = query_ref[rows, cols], grad_ref[rows, cols]
+    lax.fori_loop(0, heads, wait_kv, 0)
+
+    def source(d, h, i, qg):
+        c = h * per + i
+        query, grad = qg[c, pl.ds(0, BLK), :], qg[c, pl.ds(BLK, BLK), :]
         query_sum = None
         key_slots = {0: range(0, i + 1), 1: range(per), 2: range(i, per)}[d]
         for j in key_slots:
             at = pl.ds(j * BLK, BLK)
-            key, value, allowed = k_ref[at, cols], v_ref[at, cols], None
+            key, value, allowed = k_ref[h, at, :], v_ref[h, at, :], None
             if d == 0 and j == i:
                 limit = BLK - counts_ref[p * per + i]
                 allowed = (key_row <= query_col) & (
@@ -173,51 +186,43 @@
                 read = mask[d * per + i, at, :]
                 key, value = key * read, value * read
             query_part, key_part, value_part = tile(
-                query, grad, key, value, kt_ref[cols, at], allowed
+                query, grad, key, value, kt_ref[h, :, at], allowed
             )
             query_sum = query_part if query_sum is None else query_sum + query_part
-            dk_acc[at, cols] += key_part
-            dv_acc[at, cols] += value_part
+            dk_acc[h, at, :] += key_part
+            dv_acc[h, at, :] += value_part
         return query_sum.T * dq_scale
 
     def one_round(h, carry):
         for i in range(per):
-            rows = pl.ds(i * BLK, BLK)
-
             @pl.when(h < heads)
             def _():
                 c = h * per + i
-                cols = pl.ds(pl.multiple_of(h * HEAD, HEAD), HEAD)
 
                 @pl.when(has2)
                 def _():
-                    for copy in z_copy(c):
-                        copy.wait_recv()
+                    z_copy(c).wait_recv()
 
                     @pl.when(even)
                     def _():
-                        for copy in y_copy(c, (r2q, r2g)):
-                            copy.start()
-
-                    dq2[rows, cols] = source(2, h, i, r2q, r2g).astype(jnp.bfloat16)
+                        y_copy(c, r2).start()
+
+                    dq2[c] = source(2, h, i, r2).astype(jnp.bfloat16)
                     d2_copy(c).start()
 
-                dq0[rows, cols] = source(0, h, i, q_ref, g_ref)
+                dq0[c] = source(0, h, i, qg_ref)
 
             @pl.when((h > 0) & has1)
             def _():
                 c = (h - 1) * per + i
-                cols = pl.ds(pl.multiple_of((h - 1) * HEAD, HEAD), HEAD)
-                for copy in y_copy(c, (q_ref, g_ref)):
-                    copy.wait_recv()
-                dq1[rows, cols] = source(1, h - 1, i, r1q, r1g).astype(jnp.bfloat16)
+                y_copy(c, qg_ref).wait_recv()
+                dq1[c] = source(1, h - 1, i, r1).astype(jnp.bfloat16)
                 d1_copy(c).start()
 
         @pl.when(h > 0)
         def _():
-            cols = pl.ds(pl.multiple_of((h - 1) * HEAD, HEAD), HEAD)
-            dk_ref[:, cols] = (dk_acc[:, cols] * dq_scale).astype(jnp.bfloat16)
-            dv_ref[:, cols] = (dv_acc[:, cols] * NORM_SCALE).astype(jnp.bfloat16)
+            dk_ref[h - 1] = (dk_acc[h - 1] * dq_scale).astype(jnp.bfloat16)
+            dv_ref[h - 1] = (dv_acc[h - 1] * NORM_SCALE).astype(jnp.bfloat16)
             for store in dkv_store(h - 1):
                 store.start()
         return carry
@@ -225,28 +230,23 @@
     lax.fori_loop(0, heads + 1, one_round, 0)
 
     def finish(c, carry):
-        rows = pl.ds(pl.multiple_of(lax.rem(c, per) * BLK, BLK), BLK)
-        cols = pl.ds(pl.multiple_of(lax.div(c, per) * HEAD, HEAD), HEAD)
-
         @pl.when(back2)
         def _():
             d2_copy(c).wait_recv()
-            dq0[rows, cols] += rq2[rows, cols].astype(jnp.float32)
-            for copy in z_copy(c):
-                copy.wait_send()
+            dq0[c] += rq2[c].astype(jnp.float32)
+            z_copy(c).wait_send()
 
         @pl.when(back1)
         def _():
             d1_copy(c).wait_recv()
-            dq0[rows, cols] += rq1[rows, cols].astype(jnp.float32)
-
-        dq_ref[rows, cols] = dq0[rows, cols].astype(jnp.bfloat16)
+            dq0[c] += rq1[c].astype(jnp.float32)
+
+        dq_ref[c] = dq0[c].astype(jnp.bfloat16)
         dq_store(c).start()
 
         @pl.when(odd | has2)
         def _():
-            for copy in y_copy(c, (q_ref, g_ref)):
-                copy.wait_send()
+            y_copy(c, qg_ref).wait_send()
 
         @pl.when(has1)
         def _():
@@ -292,8 +292,10 @@
     per, heads = rows // BLK, columns // HEAD
     chunks = heads * per
     narrow = pltpu.VMEM((rows, columns), jnp.bfloat16)
-    wide = pltpu.VMEM((rows, columns), jnp.float32)
-    pair = pltpu.SemaphoreType.DMA((2, chunks))
+    by_chunk = pltpu.VMEM((chunks, BLK, HEAD), jnp.bfloat16)
+    pairs = pltpu.VMEM((chunks, 2 * BLK, HEAD), jnp.bfloat16)
+    by_head = pltpu.VMEM((heads, rows, HEAD), jnp.bfloat16)
+    head_sum = pltpu.VMEM((heads, rows, HEAD), jnp.float32)
     single = pltpu.SemaphoreType.DMA((chunks,))
     scalars = pl.BlockSpec(memory_space=pltpu.SMEM)
     result = jax.ShapeDtypeStruct((rows, columns), jnp.bfloat16)
@@ -302,12 +304,14 @@
         out_shape=(result, result, result),
         in_specs=[scalars, scalars] + [pl.BlockSpec(memory_space=pl.ANY)] * 4,
         out_specs=(pl.BlockSpec(memory_space=pl.ANY),) * 3,
-        scratch_shapes=[narrow] * 7
-        + [pltpu.VMEM((columns, rows), jnp.bfloat16)]
-        + [narrow] * 8
-        + [wide] * 3
+        scratch_shapes=[by_chunk, by_head, by_head, pairs, by_head, by_head]
+        + [pltpu.VMEM((heads, HEAD, rows), jnp.bfloat16), pairs, pairs]
+        + [by_chunk] * 4
+        + [pltpu.VMEM((chunks, BLK, HEAD), jnp.float32), head_sum, head_sum]
         + [pltpu.VMEM((3 * per, rows, HEAD), jnp.bfloat16)]
-        + [pair] * 4 + [single] * 4 + [pltpu.SemaphoreType.DMA((4,)), single, pltpu.SemaphoreType.DMA((2, heads))],
+        + [single] * 8
+        + [pltpu.SemaphoreType.DMA((2, chunks)), pltpu.SemaphoreType.DMA((2, heads))]
+        + [single, pltpu.SemaphoreType.DMA((2, heads))],
         compiler_params=pltpu.CompilerParams(
             collective_id=0, has_side_effects=True, vmem_limit_bytes=56 * 1024 * 1024
         ),

time: 65.6 us -> 65.5 us (level)
  no operation moved by 1% of the time
where the time goes in v5:
time: 65.5 us; the launch traced here: 65.3 us
  Pallas kernels  64.7 us (99%)
    pallas_call x1, Pallas kernels, near_body(): pl.pallas_call(functools.partial(kernel, n, per, heads), out_shape=(resul...  62.2 us
    pallas_call x1, Pallas kernels, near_body(): pl.pallas_call(hand_over, out_shape=(result, result, result), in_specs=[p...  2.49 us

profile of v5, /device:TPU:10, one launch (start us, length us, event | category | flops | bytes accessed | tf_op | source)
XLA Modules:
  0.0 65.3 jit_solution(9081452499996161275)
XLA Ops:
  0.6 62.2 %shard_map.85 = (bf16[768,512]{1,0:T(8,128)(2,1)}, bf16[768,512]{1,0:T(8,128)(2,1)}, bf16[768,512]{1,0:T(8,128)(2,1)}) custom-call(s32[16,24]{1,0:T(8,128)} %bitcast.1, s32[24]{0:T(128)} %counts_ref.1, bf16[768,512]{1,0:T(8,128)(2,1)} %q_hbm.1, bf16[768,512]{1,0:T(8,128)(2,1)} %g_hbm.1, bf16[768,512]{1,0:T(8,128)(2,1)} %k_hbm.1, bf16[768,512]{1,0:T(8,128)(2,1)} %v_hbm.1), custom_call_target="tpu_custom_call" | custom-call | tf_op jit(solution)/shard_map/pallas_call | solution.py:302
  62.8 2.5 %shard_map.86 = (bf16[768,512]{1,0:T(8,128)(2,1)}, bf16[768,512]{1,0:T(8,128)(2,1)}, bf16[768,512]{1,0:T(8,128)(2,1)}) custom-call(bf16[768,512]{1,0:T(8,128)(2,1)} %get-tuple-element.6.a_in, bf16[768,512]{1,0:T(8,128)(2,1)} %get-tuple-element.7.b_in, bf16[768,512]{1,0:T(8,128)(2,1)} %get-tuple-element.8.c_in), custom_call_target="tpu_custom_call" | custom-call | tf_op jit(solution)/shard_map/pallas_call | solution.py:319

commit v6 on v5

--- a/solution.py
+++ b/solution.py
@@ -40,7 +40,7 @@
     n, per, heads,
     blocks_ref, counts_ref, q_hbm, g_hbm, k_hbm, v_hbm,
     dq_hbm, dk_hbm, dv_hbm,
-    dq_ref, dk_ref, dv_ref, qg_ref, k_ref, v_ref, kt_ref, r1, r2, dq1, dq2, rq1, rq2, dq0, dk_acc, dv_acc, mask,
+    dq_ref, dk_ref, dv_ref, qg_ref, k_ref, v_ref, kt_ref, r1, r2, dq1, dq2, rq1, rq2, dq0, dk_new, dv_new, dk_old, dv_old, mask,
     z_send, z_recv, y_send, y_recv, d1_send, d1_recv, d2_send, d2_recv, qg_own, kv_own, dq_out, dkv_out,
 ):
     p = lax.axis_index("ctx")
@@ -165,11 +165,11 @@
     key_row = lax.broadcasted_iota(jnp.int32, (BLK, BLK), 0)
     query_col = lax.broadcasted_iota(jnp.int32, (BLK, BLK), 1)
 
-    dk_acc[...] = jnp.zeros_like(dk_acc)
-    dv_acc[...] = jnp.zeros_like(dv_acc)
+    dk_new[...] = jnp.zeros_like(dk_new)
+    dv_new[...] = jnp.zeros_like(dv_new)
     lax.fori_loop(0, heads, wait_kv, 0)
 
-    def source(d, h, i, qg):
+    def source(d, h, i, qg, dk_sum, dv_sum):
         c = h * per + i
         query, grad = qg[c, pl.ds(0, BLK), :], qg[c, pl.ds(BLK, BLK), :]
         query_sum = None
@@ -189,8 +189,8 @@
                 query, grad, key, value, kt_ref[h, :, at], allowed
             )
             query_sum = query_part if query_sum is None else query_sum + query_part
-            dk_acc[h, at, :] += key_part
-            dv_acc[h, at, :] += value_part
+            dk_sum[at, :] += key_part
+            dv_sum[at, :] += value_part
         return query_sum.T * dq_scale
 
     def one_round(h, carry):
@@ -207,24 +207,30 @@
                     def _():
                         y_copy(c, r2).start()
 
-                    dq2[c] = source(2, h, i, r2).astype(jnp.bfloat16)
+                    dq2[c] = source(2, h, i, r2, dk_new, dv_new).astype(jnp.bfloat16)
                     d2_copy(c).start()
 
-                dq0[c] = source(0, h, i, qg_ref)
+                dq0[c] = source(0, h, i, qg_ref, dk_new, dv_new)
 
             @pl.when((h > 0) & has1)
             def _():
                 c = (h - 1) * per + i
                 y_copy(c, qg_ref).wait_recv()
-                dq1[c] = source(1, h - 1, i, r1).astype(jnp.bfloat16)
+                part_sum = source(1, h - 1, i, r1, dk_old, dv_old)
+                dq1[c] = part_sum.astype(jnp.bfloat16)
                 d1_copy(c).start()
 
         @pl.when(h > 0)
         def _():
-            dk_ref[h - 1] = (dk_acc[h - 1] * dq_scale).astype(jnp.bfloat16)
-            dv_ref[h - 1] = (dv_acc[h - 1] * NORM_SCALE).astype(jnp.bfloat16)
+            dk_ref[h - 1] = (dk_old[...] * dq_scale).astype(jnp.bfloat16)
+            dv_ref[h - 1] = (dv_old[...] * NORM_SCALE).astype(jnp.bfloat16)
             for store in dkv_store(h - 1):
                 store.start()
+
+        dk_old[...] = dk_new[...]
+        dv_old[...] = dv_new[...]
+        dk_new[...] = jnp.zeros_like(dk_new)
+        dv_new[...] = jnp.zeros_like(dv_new)
         return carry
 
     lax.fori_loop(0, heads + 1, one_round, 0)
@@ -295,7 +301,7 @@
     by_chunk = pltpu.VMEM((chunks, BLK, HEAD), jnp.bfloat16)
     pairs = pltpu.VMEM((chunks, 2 * BLK, HEAD), jnp.bfloat16)
     by_head = pltpu.VMEM((heads, rows, HEAD), jnp.bfloat16)
-    head_sum = pltpu.VMEM((heads, rows, HEAD), jnp.float32)
+    head_sum = pltpu.VMEM((rows, HEAD), jnp.float32)
     single = pltpu.SemaphoreType.DMA((chunks,))
     scalars = pl.BlockSpec(memory_space=pltpu.SMEM)
     result = jax.ShapeDtypeStruct((rows, columns), jnp.bfloat16)
@@ -307,7 +313,8 @@
         scratch_shapes=[by_chunk, by_head, by_head, pairs, by_head, by_head]
         + [pltpu.VMEM((heads, HEAD, rows), jnp.bfloat16), pairs, pairs]
         + [by_chunk] * 4
-        + [pltpu.VMEM((chunks, BLK, HEAD), jnp.float32), head_sum, head_sum]
+        + [pltpu.VMEM((chunks, BLK, HEAD), jnp.float32)]
+        + [head_sum] * 4
         + [pltpu.VMEM((3 * per, rows, HEAD), jnp.bfloat16)]
         + [single] * 8
         + [pltpu.SemaphoreType.DMA((2, chunks)), pltpu.SemaphoreType.DMA((2, heads))]

time: 65.5 us -> 65.5 us (level)
  no operation moved by 1% of the time
where the time goes in v6:
time: 65.5 us; the launch traced here: 65.3 us
  Pallas kernels  64.7 us (99%)
    pallas_call x1, Pallas kernels, near_body(): pl.pallas_call(functools.partial(kernel, n, per, heads), out_shape=(resul...  62.2 us
    pallas_call x1, Pallas kernels, near_body(): pl.pallas_call(hand_over, out_shape=(result, result, result), in_specs=[p...  2.49 us

profile of v6, /device:TPU:10, one launch (start us, length us, event | category | flops | bytes accessed | tf_op | source)
XLA Modules:
  0.0 65.3 jit_solution(13058881177172391508)
XLA Ops:
  0.6 62.2 %shard_map.85 = (bf16[768,512]{1,0:T(8,128)(2,1)}, bf16[768,512]{1,0:T(8,128)(2,1)}, bf16[768,512]{1,0:T(8,128)(2,1)}) custom-call(s32[16,24]{1,0:T(8,128)} %bitcast.1, s32[24]{0:T(128)} %counts_ref.1, bf16[768,512]{1,0:T(8,128)(2,1)} %q_hbm.1, bf16[768,512]{1,0:T(8,128)(2,1)} %g_hbm.1, bf16[768,512]{1,0:T(8,128)(2,1)} %k_hbm.1, bf16[768,512]{1,0:T(8,128)(2,1)} %v_hbm.1), custom_call_target="tpu_custom_call" | custom-call | tf_op jit(solution)/shard_map/pallas_call | solution.py:308
  62.8 2.5 %shard_map.86 = (bf16[768,512]{1,0:T(8,128)(2,1)}, bf16[768,512]{1,0:T(8,128)(2,1)}, bf16[768,512]{1,0:T(8,128)(2,1)}) custom-call(bf16[768,512]{1,0:T(8,128)(2,1)} %get-tuple-element.6.a_in, bf16[768,512]{1,0:T(8,128)(2,1)} %get-tuple-element.7.b_in, bf16[768,512]{1,0:T(8,128)(2,1)} %get-tuple-element.8.c_in), custom_call_target="tpu_custom_call" | custom-call | tf_op jit(solution)/shard_map/pallas_call | solution.py:326

commit v7 on v6

--- a/solution.py
+++ b/solution.py
@@ -52,7 +52,10 @@
     next1, next2 = lax.rem(p + 1, n), lax.rem(p + 2, n)
     prev1, prev2 = lax.rem(p + n - 1, n), lax.rem(p + n - 2, n)
     partner = p + 1 - 2 * lax.rem(p, 2)
+    first_core = lax.rem(lax.axis_index("tp"), 2) == 0
+    second_core = lax.rem(lax.axis_index("tp"), 2) == 1
     chunks = heads * per
+    lead = min(4, chunks)
     dq_scale = 0.5 * NORM_SCALE * HEAD_FACTOR
 
     def part(ref, c):
@@ -131,20 +134,31 @@
             pl.semaphore_signal(barrier, inc=1, device_id={"ctx": to}, device_id_type=MESH)
     pl.semaphore_wait(barrier, jnp.minimum(p, 2) + jnp.minimum(n - 1 - p, 2))
 
-    def first_sends(c, carry):
+    def own_sends(c):
+        @pl.when(back2 & first_core)
+        def _():
+            z_copy(c).start()
+
+        @pl.when(odd)
+        def _():
+            y_copy(c, qg_ref).start()
+
+        @pl.when(back2 & second_core)
+        def _():
+            z_copy(c).start()
+
+    def loaded(c, carry):
         for load in qg_load(c):
             load.wait()
-
-        @pl.when(back2)
-        def _():
-            z_copy(c).start()
-
-        @pl.when(odd)
-        def _():
-            y_copy(c, qg_ref).start()
-        return carry
-
-    lax.fori_loop(0, chunks, first_sends, 0)
+        return carry
+
+    def first_sends(c, carry):
+        loaded(c, carry)
+        own_sends(c)
+        return carry
+
+    lax.fori_loop(0, lead, first_sends, 0)
+    lax.fori_loop(lead, chunks, loaded, 0)
 
     row = lax.broadcasted_iota(jnp.int32, (BLK, HEAD), 0)
     for j in range(per):
@@ -198,6 +212,11 @@
             @pl.when(h < heads)
             def _():
                 c = h * per + i
+                more = c + lead < chunks
+
+                @pl.when(more & first_core)
+                def _():
+                    own_sends(c + lead)
 
                 @pl.when(has2)
                 def _():
@@ -207,6 +226,12 @@
                     def _():
                         y_copy(c, r2).start()
 
+                @pl.when(more & second_core)
+                def _():
+                    own_sends(c + lead)
+
+                @pl.when(has2)
+                def _():
                     dq2[c] = source(2, h, i, r2, dk_new, dv_new).astype(jnp.bfloat16)
                     d2_copy(c).start()
 

time: 65.5 us -> 65.5 us (level)
  no operation moved by 1% of the time
where the time goes in v7:
time: 65.5 us; the launch traced here: 65.3 us
  Pallas kernels  64.7 us (99%)
    pallas_call x1, Pallas kernels, near_body(): pl.pallas_call(functools.partial(kernel, n, per, heads), out_shape=(resul...  62.2 us
    pallas_call x1, Pallas kernels, near_body(): pl.pallas_call(hand_over, out_shape=(result, result, result), in_specs=[p...  2.49 us

profile of v7, /device:TPU:10, one launch (start us, length us, event | category | flops | bytes accessed | tf_op | source)
XLA Modules:
  0.0 65.3 jit_solution(8458253530488839346)
XLA Ops:
  0.6 62.2 %shard_map.85 = (bf16[768,512]{1,0:T(8,128)(2,1)}, bf16[768,512]{1,0:T(8,128)(2,1)}, bf16[768,512]{1,0:T(8,128)(2,1)}) custom-call(s32[16,24]{1,0:T(8,128)} %bitcast.1, s32[24]{0:T(128)} %counts_ref.1, bf16[768,512]{1,0:T(8,128)(2,1)} %q_hbm.1, bf16[768,512]{1,0:T(8,128)(2,1)} %g_hbm.1, bf16[768,512]{1,0:T(8,128)(2,1)} %k_hbm.1, bf16[768,512]{1,0:T(8,128)(2,1)} %v_hbm.1), custom_call_target="tpu_custom_call" | custom-call | tf_op jit(solution)/shard_map/pallas_call | solution.py:333
  62.8 2.5 %shard_map.86 = (bf16[768,512]{1,0:T(8,128)(2,1)}, bf16[768,512]{1,0:T(8,128)(2,1)}, bf16[768,512]{1,0:T(8,128)(2,1)}) custom-call(bf16[768,512]{1,0:T(8,128)(2,1)} %get-tuple-element.6.a_in, bf16[768,512]{1,0:T(8,128)(2,1)} %get-tuple-element.7.b_in, bf16[768,512]{1,0:T(8,128)(2,1)} %get-tuple-element.8.c_in), custom_call_target="tpu_custom_call" | custom-call | tf_op jit(solution)/shard_map/pallas_call | solution.py:351

commit v8 on v7

--- a/solution.py
+++ b/solution.py
@@ -187,9 +187,9 @@
         c = h * per + i
         query, grad = qg[c, pl.ds(0, BLK), :], qg[c, pl.ds(BLK, BLK), :]
         query_sum = None
-        key_slots = {0: range(0, i + 1), 1: range(per), 2: range(i, per)}[d]
-        for j in key_slots:
-            at = pl.ds(j * BLK, BLK)
+        key_spans = {0: [(0, i), (i, 1)] if i else [(i, 1)], 1: [(0, per)], 2: [(i, per - i)]}
+        for j, count in key_spans[d]:
+            at = pl.ds(j * BLK, count * BLK)
             key, value, allowed = k_ref[h, at, :], v_ref[h, at, :], None
             if d == 0 and j == i:
                 limit = BLK - counts_ref[p * per + i]

time: 65.5 us -> 65.4 us (level)
  no operation moved by 1% of the time
where the time goes in v8:
time: 65.4 us; the launch traced here: 65.2 us
  Pallas kernels  64.5 us (99%)
    pallas_call x1, Pallas kernels, near_body(): pl.pallas_call(functools.partial(kernel, n, per, heads), out_shape=(resul...  62 us
    pallas_call x1, Pallas kernels, near_body(): pl.pallas_call(hand_over, out_shape=(result, result, result), in_specs=[p...  2.49 us

profile of v8, /device:TPU:10, one launch (start us, length us, event | category | flops | bytes accessed | tf_op | source)
XLA Modules:
  0.0 65.2 jit_solution(17294106932668916065)
XLA Ops:
  0.6 62.0 %shard_map.85 = (bf16[768,512]{1,0:T(8,128)(2,1)}, bf16[768,512]{1,0:T(8,128)(2,1)}, bf16[768,512]{1,0:T(8,128)(2,1)}) custom-call(s32[16,24]{1,0:T(8,128)} %bitcast.1, s32[24]{0:T(128)} %counts_ref.1, bf16[768,512]{1,0:T(8,128)(2,1)} %q_hbm.1, bf16[768,512]{1,0:T(8,128)(2,1)} %g_hbm.1, bf16[768,512]{1,0:T(8,128)(2,1)} %k_hbm.1, bf16[768,512]{1,0:T(8,128)(2,1)} %v_hbm.1), custom_call_target="tpu_custom_call" | custom-call | tf_op jit(solution)/shard_map/pallas_call | solution.py:333
  62.7 2.5 %shard_map.86 = (bf16[768,512]{1,0:T(8,128)(2,1)}, bf16[768,512]{1,0:T(8,128)(2,1)}, bf16[768,512]{1,0:T(8,128)(2,1)}) custom-call(bf16[768,512]{1,0:T(8,128)(2,1)} %get-tuple-element.6.a_in, bf16[768,512]{1,0:T(8,128)(2,1)} %get-tuple-element.7.b_in, bf16[768,512]{1,0:T(8,128)(2,1)} %get-tuple-element.8.c_in), custom_call_target="tpu_custom_call" | custom-call | tf_op jit(solution)/shard_map/pallas_call | solution.py:351
